TPU v7x, 256 devices: a whole 4x4x8 slice. The times are simulated.
256 devices in a mesh: fsdp: 32 (over z, y_hi, core), tp: 8 (over x, y_lo).
Axes of the slice: x: 4, y: 4 (y_hi: 2, y_lo: 2; y = y_hi * 2 + y_lo), z: 8, core: 2. Of those that a mesh axis runs over, the one named last changes fastest.
Arguments:
- patches: bfloat16 [14336, 3072], P('fsdp'), may hold values from -500 to 500
- cotangent: bfloat16 [14336, 3072], P('fsdp'), may hold values from -6 to 6
- counts: int32 [32, 4], replicated, may hold values from 32 to 112, as said below
- masks: int32 [4], replicated, may hold values from 0 to 31, as said below
- norm_gain: float32 [3072], replicated, may hold values from 0.25 to 1.75
- qk_gain: float32 [2, 128], replicated, may hold values from 0.25 to 1.75
- qkv_weight: bfloat16 [3072, 9216], P('fsdp', 'tp'), may hold values from -0.109375 to 0.109375
- out_weight: bfloat16 [3072, 3072], P('fsdp', 'tp'), may hold values from -0.109375 to 0.109375
Outputs:
- attended: bfloat16 [14336, 3072], P('fsdp', 'tp')
- grad_rows: bfloat16 [14336, 3072], P('fsdp', 'tp')
- grad_qkv_weight: float32 [3072, 9216], P('fsdp', 'tp')
- grad_out_weight: float32 [3072, 3072], P('fsdp', 'tp')
Inputs may be any that keep to these rules, and one draw needn't show every extreme that they name: `masks`: in every draw some slot's mask is 31. `counts`: in every draw some run block holds 112 patches in each of its slots.
All inputs are finite; a program needn't handle non-finite values.
Results may differ from a plain program's by a relative error of at most 0.02.
Values may be sent and summed in bfloat16 or wider, within the bound.
A program may use at most 128 MiB of HBM per device.

v0:
```python
import jax
import jax.numpy as jnp
from jax import lax
from jax.sharding import PartitionSpec as P

epsilon = 1e-06


def partner_2(value, axis, stride):
    mask = 2**stride
    pairs = [(source, source ^ mask) for source in range(lax.axis_size(axis))]
    return lax.ppermute(value, axis, pairs)


def norm_rows(values):
    row_mean = jnp.mean(values, axis=-1, keepdims=True)
    centred = values - row_mean
    factor = lax.rsqrt(jnp.mean(centred * centred, axis=-1, keepdims=True) + epsilon)
    return (centred * factor, factor)


def norm_back(upstream, normed, factor):
    return factor * (
        upstream
        - jnp.mean(upstream, axis=-1, keepdims=True)
        - normed * jnp.mean(upstream * normed, axis=-1, keepdims=True)
    )


def per_device(patches, cotangent, counts, masks, norm_gain, qk_gain, qkv_weight, out_weight):
    replicas = lax.axis_size("fsdp")
    groups = lax.axis_size("tp")
    my_replica = lax.axis_index("fsdp")
    my_group = lax.axis_index("tp")
    tok_rows = patches.shape[0]
    images = counts.shape[1]
    slot_rows = tok_rows // images
    model_width = norm_gain.shape[0]
    share_width = model_width // groups
    head_dim = qk_gain.shape[1]
    qkv_cols = qkv_weight.shape[1]
    out_cols = out_weight.shape[1]
    local_heads = out_cols // head_dim
    row_slot = jnp.arange(tok_rows, dtype=jnp.int32) // slot_rows
    holding = lax.dynamic_slice_in_dim(patches, my_group * share_width, share_width, 1)
    digit_count = replicas.bit_length() - 1
    digit_order = list(range(digit_count))
    for bit_place in digit_order:
        partner = partner_2(holding, "fsdp", bit_place)
        moving = jnp.bitwise_and(jnp.right_shift(masks, bit_place), 1) == 1
        take_rows = jnp.take(moving, row_slot)
        holding = jnp.where(take_rows[:, None], partner, holding)
    replica_ids = jnp.arange(replicas, dtype=jnp.int32)
    sources = jnp.bitwise_xor(my_replica, masks)
    run_counts = jnp.sum(jnp.where(replica_ids[:, None] == sources[None, :], counts, 0), axis=0)
    places = jnp.arange(slot_rows, dtype=jnp.int32)
    live_slots = places[None, :] < run_counts[:, None]
    is_live = live_slots.reshape(tok_rows)
    allowed = live_slots[:, :, None] & live_slots[:, None, :] | jnp.eye(slot_rows, dtype=bool)[None]
    packed = jnp.where(is_live[:, None], holding, jnp.zeros((), holding.dtype))
    block_rows = lax.all_gather(packed, "tp", axis=1, tiled=True)
    qkv_full, out_full = (
        lax.all_gather(qkv_weight, "fsdp", axis=0, tiled=True),
        lax.all_gather(out_weight, "fsdp", axis=0, tiled=True),
    )
    centred_rows, row_factor = norm_rows(block_rows.astype(jnp.float32))
    normed = (centred_rows * norm_gain).astype(jnp.bfloat16)
    projected = jnp.dot(normed, qkv_full, preferred_element_type=jnp.float32).reshape(
        images, slot_rows, local_heads, 3, head_dim
    )
    query_hat, query_factor = norm_rows(projected[:, :, :, 0])
    key_hat, key_factor = norm_rows(projected[:, :, :, 1])
    query_scale = qk_gain[0] * head_dim ** (-0.5)
    key_scale = qk_gain[1]
    query = (query_hat * query_scale).astype(jnp.bfloat16)
    key_rows = (key_hat * key_scale).astype(jnp.bfloat16)
    values = projected[:, :, :, 2].astype(jnp.bfloat16)
    scores = jnp.einsum("sqhe,skhe->shqk", query, key_rows, preferred_element_type=jnp.float32)
    raised = jnp.where(allowed[:, None], jnp.exp(scores), 0.0)
    attention = raised / jnp.sum(raised, axis=-1, keepdims=True)
    rounded_attention = attention.astype(jnp.bfloat16)
    mixed = jnp.einsum(
        "shqk,skhe->sqhe", rounded_attention, values, preferred_element_type=jnp.float32
    )
    mixed = mixed.astype(jnp.bfloat16).reshape(tok_rows, out_cols)
    partial_value = lax.dot_general(
        mixed, out_full, (((1,), (1,)), ((), ())), preferred_element_type=jnp.float32
    )
    attended = lax.psum_scatter(
        partial_value.astype(jnp.bfloat16), "tp", scatter_dimension=1, tiled=True
    ).astype(jnp.float32)
    attended = jnp.where(is_live[:, None], attended, 0.0).astype(jnp.bfloat16)
    upstream_rows = jnp.where(is_live[:, None], cotangent, jnp.zeros((), cotangent.dtype))
    grad_mixed = jnp.dot(upstream_rows, out_full, preferred_element_type=jnp.float32).astype(
        jnp.bfloat16
    )
    grad_heads = grad_mixed.reshape(images, slot_rows, local_heads, head_dim)
    grad_value = jnp.einsum(
        "shqk,sqhe->skhe", rounded_attention, grad_heads, preferred_element_type=jnp.float32
    )
    grad_attention = jnp.einsum(
        "sqhe,skhe->shqk", grad_heads, values, preferred_element_type=jnp.float32
    )
    grad_scores = attention * (
        grad_attention - jnp.sum(attention * grad_attention, axis=-1, keepdims=True)
    )
    grad_scores = grad_scores.astype(jnp.bfloat16)
    grad_query = jnp.einsum(
        "shqk,skhe->sqhe", grad_scores, key_rows, preferred_element_type=jnp.float32
    )
    grad_key = jnp.einsum("shqk,sqhe->skhe", grad_scores, query, preferred_element_type=jnp.float32)
    query_grad = norm_back(grad_query * query_scale, query_hat, query_factor)
    key_grad = norm_back(grad_key * key_scale, key_hat, key_factor)
    grad_qkv = (
        jnp.stack([query_grad, key_grad, grad_value], axis=3)
        .astype(jnp.bfloat16)
        .reshape(tok_rows, qkv_cols)
    )
    qkv_term = lax.dot_general(
        normed, grad_qkv, (((0,), (0,)), ((), ())), preferred_element_type=jnp.float32
    )
    out_term = lax.dot_general(
        upstream_rows, mixed, (((0,), (0,)), ((), ())), preferred_element_type=jnp.float32
    )
    stacked = lax.psum_scatter(
        jnp.concatenate([qkv_term, out_term], axis=1).astype(jnp.bfloat16),
        "fsdp",
        scatter_dimension=0,
        tiled=True,
    ).astype(jnp.float32)
    grad_qkv_weight = stacked[:, :qkv_cols]
    grad_out_weight = stacked[:, qkv_cols:]
    partial_back = lax.dot_general(
        grad_qkv, qkv_full, (((1,), (1,)), ((), ())), preferred_element_type=jnp.float32
    )
    summed = lax.psum(partial_back.astype(jnp.bfloat16), "tp").astype(jnp.float32)
    grad_full = norm_back(summed * norm_gain, centred_rows, row_factor)
    grad_share = lax.dynamic_slice_in_dim(grad_full, my_group * share_width, share_width, 1)
    grad_rows = grad_share.astype(jnp.bfloat16)
    return (attended, grad_rows, grad_qkv_weight, grad_out_weight)


def solution(mesh):
    in_specs = (
        P("fsdp", None),
        P("fsdp", None),
        P(),
        P(),
        P(),
        P(),
        P("fsdp", "tp"),
        P("fsdp", "tp"),
    )
    out_specs = (P("fsdp", "tp"), P("fsdp", "tp"), P("fsdp", "tp"), P("fsdp", "tp"))
    return jax.shard_map(
        per_device, mesh=mesh, in_specs=in_specs, out_specs=out_specs, check_vma=False
    )
```

profile of v0, /device:TPU:2, one launch (start us, length us, event | category | flops | bytes accessed | tf_op | source)
XLA Modules:
  0.0 702.9 jit_solution(246220359881988830)
XLA Ops:
  7.2 0.7 all-gather.8.cloned.1.call-update
  8.0 1.0 constant_dynamic-slice_fusion
  10.4 2.6 select_select_fusion.1
  13.0 1.2 broadcast_select_fusion.3
  14.2 3.3 collective-permute-start.1
  18.1 2.5 select_select_fusion.2
  20.7 5.6 collective-permute-done.1
  26.4 2.0 collective-permute-start.2
  28.4 2.6 select_select_fusion.3
  31.0 6.3 collective-permute-done.2
  37.5 3.0 collective-permute-start.3
  41.1 2.5 select_select_fusion.4
  43.6 13.2 %collective-permute-done.3 = bf16[448,384]{1,0:T(8,128)(2,1)S(1)} collective-permute-done((bf16[448,384]{1,0:T(8,128)(2,1)S(1)}, bf16[448,384]{1,0:T(8,128)(2,1)S(1)}, u32[]{:S(2)}, u32[]{:S(2)}) %collective-permute-start.3) | collective-permute-done | bytes 344096 | tf_op jit(solution)/shard_map/ppermute | solution.py:12
  57.0 5.6 collective-permute-start.4
  62.9 2.6 select_select_fusion.5
  65.5 12.8 %collective-permute-done.4 = bf16[448,384]{1,0:T(8,128)(2,1)S(1)} collective-permute-done((bf16[448,384]{1,0:T(8,128)(2,1)S(1)}, bf16[448,384]{1,0:T(8,128)(2,1)S(1)}, u32[]{:S(2)}, u32[]{:S(2)}) %collective-permute-start.4) | collective-permute-done | bytes 344096 | tf_op jit(solution)/shard_map/ppermute | solution.py:12
  78.3 0.9 select_select_fusion
  79.3 0.7 all-gather.6.cloned.1.call-update
  80.3 21.2 %all-gather.8.cloned.1.call-done = bf16[3072,384]{1,0:T(8,128)(2,1)} async-done(((bf16[96,384]{1,0:T(8,128)(2,1)}), bf16[3072,384]{1,0:T(8,128)(2,1)}) %all-gather.8.cloned.1.call-update) | async-done | bytes 2359312 | tf_op jit(solution)/shard_map/all_gather | solution.py:64
  101.5 4.1 convolution_convert_fusion.4
  105.6 0.9 reshape.244
  106.5 60.2 %all-gather.4.cloned.1.call-done = bf16[448,3072]{1,0:T(8,128)(2,1)} async-done(((bf16[448,384]{1,0:T(8,128)(2,1)}), bf16[448,3072]{1,0:T(8,128)(2,1)}) %all-gather.4.cloned.1.call-update) | async-done | bytes 2752528 | tf_op jit(solution)/shard_map/all_gather | solution.py:61
  166.7 2.4 convert_reduce_fusion
  169.3 0.9 fusion.2
  170.2 96.7 %all-gather.6.cloned.1.call-done = bf16[3072,1152]{1,0:T(8,128)(2,1)} async-done(((bf16[96,1152]{1,0:T(8,128)(2,1)}), bf16[3072,1152]{1,0:T(8,128)(2,1)}) %all-gather.6.cloned.1.call-update) | async-done | bytes 7077904 | tf_op jit(solution)/shard_map/all_gather | solution.py:63
  266.9 8.5 %fusion.9 = f32[448,1152]{0,1:T(8,128)} fusion(bf16[3072,1152]{1,0:T(8,128)(2,1)} %all-gather.6.cloned.1.call-done, f32[3072]{0:T(1024)S(1)} %copy-done.5, bf16[448,3072]{1,0:T(8,128)(2,1)S(1)} %copy-done, f32[448]{0:T(512)S(1)} %add_rsqrt_fusion.2, f32[448]{0:T(512)S(1)} %broadcast_multiply_fusion.8), kind=kOutput, calls=%fused_computation.26 | convolution fusion | flops 3177775104 | bytes 11910656 | tf_op jit(solution)/shard_map/dot_general | solution.py:68
  275.3 4.1 reshape.161
  279.4 1.3 slice.74
  280.7 3.0 fusion.37
  283.7 1.0 copy.59
  284.6 1.4 copy.57
  286.6 2.2 copy.58
  288.8 1.6 multiply_reduce_fusion.4
  290.4 2.3 fusion.17
  292.8 3.1 multiply_reduce_fusion.3
  295.9 1.6 fusion.8
  297.5 1.4 multiply_convert_fusion.5
  298.9 2.0 fusion.36
  300.9 2.0 fusion.35
  303.0 0.9 fusion.16
  303.9 0.9 fusion.15
  304.7 1.1 pad_maximum_fusion.1
  305.8 3.3 copy.44
  309.2 3.3 convert_element_type.71
  312.5 9.1 %convolution_convert_fusion.1 = bf16[448,3072]{1,0:T(8,128)(2,1)} fusion(bf16[448,1152]{0,1:T(8,128)(2,1)} %convert_element_type.71, bf16[3072,1152]{1,0:T(8,128)(2,1)} %all-gather.6.cloned.1.call-done), kind=kOutput, calls=%fused_computation.10 | convolution fusion | flops 3172270080 | bytes 10862592 | tf_op jit(solution)/shard_map/dot_general | solution.py:133
  321.9 0.8 copy-done.2
  322.7 2.0 fusion.7
  324.7 1.2 copy.39
  326.2 4.9 convolution_convert_fusion.2
  331.1 4.6 copy.53
  336.3 3.3 convolution_convert_fusion.3
  339.7 4.3 convolution_convert_fusion
  344.0 9.8 %pad_maximum_fusion = bf16[3072,1536]{0,1:T(8,128)(2,1)} fusion(bf16[3072,384]{0,1:T(8,128)(2,1)S(1)} %convolution_convert_fusion.3, bf16[3072,1152]{0,1:T(8,128)(2,1)S(1)} %convolution_convert_fusion), kind=kLoop, calls=%fused_computation.1 | loop fusion | flops 18874368 | bytes 18874368 | tf_op jit(solution)/shard_map/concatenate | solution.py:126
  353.9 12.7 %copy.55 = bf16[3072,1536]{1,0:T(8,128)(2,1)} copy(bf16[3072,1536]{0,1:T(8,128)(2,1)} %pad_maximum_fusion) | data formatting | bytes 18874368
  366.6 85.1 %all-reduce.2.cloned.1.call-done = bf16[448,3072]{1,0:T(8,128)(2,1)} async-done(((bf16[448,3072]{1,0:T(8,128)(2,1)}), bf16[448,3072]{1,0:T(8,128)(2,1)}) %all-reduce.2.cloned.1.call-update) | async-done | bytes 2752528 | tf_op jit(solution)/shard_map/psum | solution.py:136
  451.7 3.4 fusion.3
  455.1 1.0 fusion.12
  456.1 72.3 %reduce-scatter.7.cloned.1.call-done = bf16[384,448]{1,0:T(8,128)(2,1)} async-done(((bf16[3072,448]{1,0:T(8,128)(2,1)}), bf16[384,448]{1,0:T(8,128)(2,1)}) %reduce-scatter.7.cloned.1.call-update) | async-done | bytes 344080
  528.4 1.2 copy.54
  529.6 0.9 select_convert_fusion
  530.5 162.3 %reduce-scatter.9.cloned.1.call-done = bf16[96,1536]{1,0:T(8,128)(2,1)} async-done(((bf16[3072,1536]{1,0:T(8,128)(2,1)}), bf16[96,1536]{1,0:T(8,128)(2,1)}) %reduce-scatter.9.cloned.1.call-update) | async-done | bytes 294928
  692.8 1.0 slice.77
  694.1 1.0 copy.45
  695.3 0.8 copy.46
  (66 shorter events, 6.1 us)
Async XLA Ops:
  7.2 36.5 %copy-start.11 = (s32[4]{0:T(128)S(1)}, s32[4]{0:T(128)}, u32[]{:S(2)}) copy-start(s32[4]{0:T(128)} %param.13) | copy-start | bytes 52
  7.2 55.4 %copy-start.9 = (s32[32,4]{0,1:T(4,128)S(1)}, s32[32,4]{0,1:T(4,128)}, u32[]{:S(2)}) copy-start(s32[32,4]{0,1:T(4,128)} %param.12) | copy-start | bytes 1540
  7.2 94.3 %all-gather.8.cloned.1.call-start = ((), (), s32[]{:S(2)}) async-start(), calls=%async_computation.4 | async-start | bytes 2433024 | tf_op jit(solution)/shard_map/all_gather | solution.py:64
  7.9 158.8 %all-gather.4.cloned.1.call-start = ((), (), s32[]{:S(2)}) async-start(), calls=%async_computation.2 | async-start | bytes 3096576 | tf_op jit(solution)/shard_map/all_gather | solution.py:61
  9.0 4.0 collective-permute-start
  13.0 67.1 %copy-start.10 = (f32[2,128]{1,0:T(2,128)S(1)}, f32[2,128]{1,0:T(2,128)}, u32[]{:S(2)}) copy-start(f32[2,128]{1,0:T(2,128)} %param.15) | copy-start | bytes 3076
  14.2 12.1 %collective-permute-start.1 = (bf16[448,384]{1,0:T(8,128)(2,1)S(1)}, bf16[448,384]{1,0:T(8,128)(2,1)S(1)}, u32[]{:S(2)}, u32[]{:S(2)}) collective-permute-start(bf16[448,384]{1,0:T(8,128)(2,1)S(1)} %broadcast_select_fusion.3), channel_id=1, source_target_pairs={{0,16},{8,24},{16,0},{24,8},{32,48},{40,56},{48,32},{56,40},{64,80... | collective-permute-start | bytes 1032200 | tf_op jit(solution)/shard_map/ppermute | solution.py:12
  26.4 10.9 %collective-permute-start.2 = (bf16[448,384]{1,0:T(8,128)(2,1)S(1)}, bf16[448,384]{1,0:T(8,128)(2,1)S(1)}, u32[]{:S(2)}, u32[]{:S(2)}) collective-permute-start(bf16[448,384]{1,0:T(8,128)(2,1)S(1)} %broadcast_select_fusion.4), channel_id=1, source_target_pairs={{0,32},{8,40},{16,48},{24,56},{32,0},{40,8},{48,16},{56,24},{64,96... | collective-permute-start | bytes 1032200 | tf_op jit(solution)/shard_map/ppermute | solution.py:12
  37.5 19.4 %collective-permute-start.3 = (bf16[448,384]{1,0:T(8,128)(2,1)S(1)}, bf16[448,384]{1,0:T(8,128)(2,1)S(1)}, u32[]{:S(2)}, u32[]{:S(2)}) collective-permute-start(bf16[448,384]{1,0:T(8,128)(2,1)S(1)} %broadcast_select_fusion.5), channel_id=1, source_target_pairs={{0,64},{8,72},{16,80},{24,88},{32,96},{40,104},{48,112},{56,120},{... | collective-permute-start | bytes 1032200 | tf_op jit(solution)/shard_map/ppermute | solution.py:12
  57.0 21.3 %collective-permute-start.4 = (bf16[448,384]{1,0:T(8,128)(2,1)S(1)}, bf16[448,384]{1,0:T(8,128)(2,1)S(1)}, u32[]{:S(2)}, u32[]{:S(2)}) collective-permute-start(bf16[448,384]{1,0:T(8,128)(2,1)S(1)} %broadcast_select_fusion.6), channel_id=1, source_target_pairs={{0,128},{8,136},{16,144},{24,152},{32,160},{40,168},{48,176},{56,1... | collective-permute-start | bytes 1032200 | tf_op jit(solution)/shard_map/ppermute | solution.py:12
  62.9 42.7 %copy-start.7 = (pred[448]{0:T(512)(128)(4,1)}, pred[448]{0:T(512)(128)(4,1)S(1)}, u32[]{:S(2)}) copy-start(pred[448]{0:T(512)(128)(4,1)S(1)} %lt.41) | copy-start | bytes 1348
  79.3 187.6 %all-gather.6.cloned.1.call-start = ((), (), s32[]{:S(2)}) async-start(), calls=%async_computation.3 | async-start | bytes 7299072 | tf_op jit(solution)/shard_map/all_gather | solution.py:63
  80.0 371.7 %all-reduce.2.cloned.1.call-start = ((), (), s32[]{:S(2)}) async-start(), calls=%async_computation.5 | async-start | bytes 5505024 | tf_op jit(solution)/shard_map/psum | solution.py:136
  166.7 2.6 copy-start
  166.7 100.1 %copy-start.5 = (f32[3072]{0:T(1024)S(1)}, f32[3072]{0:T(1024)}, u32[]{:S(2)}) copy-start(f32[3072]{0:T(1024)} %param.14) | copy-start | bytes 36868
  295.9 3.0 copy-start.1
  321.6 1.1 copy-start.2
  321.6 206.8 %reduce-scatter.7.cloned.1.call-start = ((), (), s32[]{:S(2)}) async-start(), calls=%async_computation.6 | async-start | bytes 3538944
  335.7 0.7 copy-start.8
  335.7 4.0 copy-start.6
  335.7 357.1 %reduce-scatter.9.cloned.1.call-start = ((), (), s32[]{:S(2)}) async-start(), calls=%async_computation.7 | async-start | bytes 9732096
  336.3 3.3 copy-start.4
  692.8 2.3 copy-start.3
Sparse Core Ops, SparseCore 0:
  10.8 90.6 all-gather.7
  103.9 62.7 all-gather.3
  169.5 97.3 all-gather.5
  321.7 129.9 all-reduce.1
  454.3 74.0 reduce-scatter.6
  533.3 159.4 reduce-scatter.8
where the time goes:
time: 704 us; the launch traced here: 703 us
  waiting for transfers between devices  537 us (76%)
  matrix products  47.3 us (7%)
  local copies, waits for them, and re-layouts  45.4 us (6%)
  other arithmetic  44.1 us (6%)
  between operations  14.5 us (2%)
  starting transfers between devices  14.4 us (2%)
    unnamed x8, waiting for transfers between devices  236 us
    all_gather x1, waiting for transfers between devices, per_device(): lax.all_gather(qkv_weight, 'fsdp', axis=0, tiled=True)  96.7 us
    psum x1, waiting for transfers between devices, per_device(): lax.psum(partial_back.astype(jnp.bfloat16), 'tp').astype(jnp.float32)  85.1 us
    all_gather x1, waiting for transfers between devices, per_device(): block_rows = lax.all_gather(packed, 'tp', axis=1, tiled=True)  60.2 us
    ppermute x5, waiting for transfers between devices, partner_2(): return lax.ppermute(value, axis, pairs)  37.9 us
    unnamed x34, local copies, waits for them, and re-layouts  27 us
    all_gather x1, waiting for transfers between devices, per_device(): lax.all_gather(out_weight, 'fsdp', axis=0, tiled=True)  21.2 us
  transfers between devices with their start and end apart: 11, of which 10 were waited for; matrix products, arithmetic and copies ran while one was open for 11% of the time, Pallas kernels for 0%

commit v1 on v0

--- a/solution.py
+++ b/solution.py
@@ -1,15 +1,521 @@
+import functools
 import jax
 import jax.numpy as jnp
 from jax import lax
+from jax.experimental import pallas as pl
+from jax.experimental.pallas import tpu as pltpu
 from jax.sharding import PartitionSpec as P
 
+MESH = pl.DeviceIdType.MESH
 epsilon = 1e-06
-
-
-def partner_2(value, axis, stride):
-    mask = 2**stride
-    pairs = [(source, source ^ mask) for source in range(lax.axis_size(axis))]
-    return lax.ppermute(value, axis, pairs)
+NZ, NX = 8, 4
+
+
+def coords():
+    f = lax.axis_index("fsdp")
+    t = lax.axis_index("tp")
+    z, yh, c = lax.div(f, 4), lax.rem(lax.div(f, 2), 2), lax.rem(f, 2)
+    x, yl = lax.div(t, 2), lax.rem(t, 2)
+    return z, yh, c, x, yl
+
+
+def dev(z, yh, c, x, yl):
+    return (z * 4 + yh * 2 + c, x * 2 + yl)
+
+
+def remote(src, dst, sems, slot, target):
+    send, recv = sems
+    return pltpu.make_async_remote_copy(
+        src_ref=src,
+        dst_ref=dst,
+        send_sem=send.at[slot],
+        recv_sem=recv.at[slot],
+        device_id=target,
+        device_id_type=MESH,
+    )
+
+
+def greet(partners):
+    barrier = pltpu.get_barrier_semaphore()
+    for partner in partners:
+        pl.semaphore_signal(barrier, inc=1, device_id=partner, device_id_type=MESH)
+    pl.semaphore_wait(barrier, len(partners))
+
+
+def gather_kernel(
+    bits_ref, live_ref, patches, qkv_w, out_w, rows, weights,
+    hold, got, a_send, a_recv, b_send, b_recv, c_send, c_recv, local_sem,
+):
+    z, yh, c, x, yl = coords()
+    me = dev(z, yh, c, x, yl)
+    f, t = me
+    slots, slot_rows, share = hold.shape[1], hold.shape[2], hold.shape[3]
+    qkv_cols = qkv_w.shape[1]
+    z_up, z_down = lax.rem(z + 1, NZ), lax.rem(z + NZ - 1, NZ)
+    x_up, x_down = lax.rem(x + 1, NX), lax.rem(x + NX - 1, NX)
+    low4, low2 = lax.rem(z, 4), lax.rem(z, 2)
+    across = dev(z, 1 - yh, c, x, 1 - yl)
+    z7 = dev(7 - z, yh, c, x, yl)
+    z3 = dev(z + 3 - 2 * low4, yh, c, x, yl)
+    z1 = dev(z + 1 - 2 * low2, yh, c, x, yl)
+    sibling = dev(z, yh, 1 - c, x, yl)
+    opposite = dev(z, 1 - yh, c, x, yl)
+    beside = dev(z, yh, c, x, 1 - yl)
+    up, down = dev(z_up, yh, c, x, yl), dev(z_down, yh, c, x, yl)
+    right, left = dev(z, yh, c, x_up, yl), dev(z, yh, c, x_down, yl)
+    greet([across, z7, z3, z1, sibling, opposite, beside, up, down, right, left])
+
+    sent = []
+
+    def go(copy):
+        copy.start()
+        sent.append(copy)
+
+    a_sems, b_sems, c_sems = (a_send, a_recv), (b_send, b_recv), (c_send, c_recv)
+
+    def columns(index):
+        return pl.ds(pl.multiple_of(index * share, 128), share)
+
+    def slot_at(k):
+        return pl.ds(k * slot_rows, slot_rows)
+
+    for k in range(slots):
+        go(remote(patches.at[slot_at(k), columns(x * 2 + 1 - yl)], got.at[0, k], a_sems, k, across))
+    own = [
+        pltpu.make_async_copy(patches.at[slot_at(k), columns(t)], hold.at[0, k], local_sem.at[k])
+        for k in range(slots)
+    ]
+    own_w = [
+        pltpu.make_async_copy(qkv_w, weights.at[f, :, pl.ds(0, qkv_cols)], local_sem.at[slots]),
+        pltpu.make_async_copy(
+            out_w, weights.at[f, :, pl.ds(qkv_cols, weights.shape[2] - qkv_cols)],
+            local_sem.at[slots + 1],
+        ),
+    ]
+    for copy in own_w + own:
+        copy.start()
+    for copy in own_w:
+        copy.wait()
+
+    def weight_copy(piece, slot, target):
+        return remote(weights.at[piece], weights.at[piece], c_sems, slot, target)
+
+    def fid(zz, kind):
+        return zz * 4 + (yh if kind == 0 else 1 - yh) * 2 + c
+
+    def sib_id(zz, kind):
+        return zz * 4 + (yh if kind == 0 else 1 - yh) * 2 + 1 - c
+
+    limits = {(0, 0): 4, (0, 1): 3, (1, 0): 3, (1, 1): 4}
+    z_slot = {}
+    for direction in range(2):
+        for kind in range(2):
+            for d in range(1, limits[direction, kind] + 1):
+                z_slot[direction, kind, d] = 1 + len(z_slot)
+    pieces = [(0, 0), (0, 1)]
+    core_slot = {}
+
+    def core_index(key):
+        if key not in core_slot:
+            core_slot[key] = 15 + len(core_slot)
+        return core_slot[key]
+
+    def z_at(distance):
+        return lax.rem(z + distance + NZ, NZ)
+
+    def share_core(distance, kind):
+        go(weight_copy(fid(z_at(distance), kind), core_index((distance, kind)), sibling))
+
+    def z_send(direction, kind, distance_travelled):
+        source = z_at(-distance_travelled if direction == 0 else distance_travelled)
+        go(
+            weight_copy(
+                fid(source, kind), z_slot[direction, kind, distance_travelled + 1],
+                up if direction == 0 else down,
+            )
+        )
+
+    def z_receive(direction, kind, d):
+        signed = -d if direction == 0 else d
+        weight_copy(fid(z_at(signed), kind), z_slot[direction, kind, d], up).wait_recv()
+        if d < limits[direction, kind]:
+            z_send(direction, kind, d)
+        share_core(signed, kind)
+
+    go(weight_copy(f, 0, opposite))
+    share_core(0, 0)
+
+    for copy in own:
+        copy.wait()
+
+    partner = {3: z3, 7: z7, 1: z1, 0: sibling}
+    column = {7: 1, 3: 2, 1: 3, 0: 4}
+    order = [[7, 3, 1, 0], [3, 7, 1, 0], [7, 3, 1, 0], [3, 7, 1, 0]]
+
+    def merge(k, step, bit_column):
+        remote(got.at[step, k], got.at[step, k], a_sems, step * slots + k, sibling).wait_recv()
+        taken = bits_ref[k, bit_column] > 0
+        return lax.select_n(taken, hold[step, k], got[step, k])
+
+    for step in range(4):
+        for k in range(slots):
+            which = order[k][step]
+            before = 0 if step == 0 else column[order[k][step - 1]]
+            hold[step + 1, k] = merge(k, step, before)
+            go(
+                remote(
+                    hold.at[step + 1, k], got.at[step + 1, k], a_sems,
+                    (step + 1) * slots + k, partner[which],
+                )
+            )
+        if step == 0:
+            z_send(0, 0, 0)
+            z_send(1, 0, 0)
+            weight_copy(fid(z, 1), 0, opposite).wait_recv()
+            z_send(0, 1, 0)
+            z_send(1, 1, 0)
+            share_core(0, 1)
+
+    def row_copy(k, xx, y_low, which, target):
+        view = rows.at[slot_at(k), columns(xx * 2 + y_low)]
+        return remote(view, view, b_sems, k * 7 + which, target)
+
+    for k in range(slots):
+        merged = merge(k, 4, column[order[k][3]]).astype(jnp.float32)
+        place = lax.broadcasted_iota(jnp.int32, (slot_rows, share), 0)
+        live = place < live_ref[k]
+        rows[slot_at(k), columns(t)] = jnp.where(live, merged, 0.0).astype(rows.dtype)
+        go(row_copy(k, x, yl, 0, beside))
+        go(row_copy(k, x, yl, 1, right))
+        go(row_copy(k, x, yl, 4, left))
+
+    def rows_second(k):
+        row_copy(k, x, 1 - yl, 0, beside).wait_recv()
+        go(row_copy(k, x, 1 - yl, 3, right))
+        go(row_copy(k, x, 1 - yl, 5, left))
+
+    def rows_third(k):
+        row_copy(k, x_down, yl, 1, right).wait_recv()
+        go(row_copy(k, x_down, yl, 2, right))
+        row_copy(k, x_up, 1 - yl, 5, left).wait_recv()
+        go(row_copy(k, x_up, 1 - yl, 6, left))
+
+    for d in range(1, 5):
+        for kind in range(2):
+            for direction in range(2):
+                if d <= limits[direction, kind]:
+                    z_receive(direction, kind, d)
+        if d == 1:
+            for k in range(slots):
+                rows_second(k)
+                rows_third(k)
+    for k in range(slots):
+        row_copy(k, lax.rem(x + 2, NX), yl, 2, right).wait_recv()
+        row_copy(k, x_down, 1 - yl, 3, right).wait_recv()
+        row_copy(k, x_up, yl, 4, left).wait_recv()
+        row_copy(k, lax.rem(x + 2, NX), 1 - yl, 6, left).wait_recv()
+    for (distance, kind), slot in core_slot.items():
+        weight_copy(sib_id(z_at(distance), kind), slot, sibling).wait_recv()
+    for copy in sent:
+        copy.wait_send()
+
+
+def gather(bits, live, patches, qkv_w, out_w):
+    tok, model = patches.shape
+    slots = bits.shape[0]
+    share = model // 8
+    slot_rows = tok // slots
+    bf16 = jnp.bfloat16
+    depth, wide = qkv_w.shape[0], qkv_w.shape[1] + out_w.shape[1]
+    hbm = pl.BlockSpec(memory_space=pl.ANY)
+    smem = pl.BlockSpec(memory_space=pltpu.SMEM)
+    return pl.pallas_call(
+        gather_kernel,
+        out_shape=(
+            jax.ShapeDtypeStruct((tok, model), bf16),
+            jax.ShapeDtypeStruct((32, depth, wide), bf16),
+        ),
+        in_specs=[smem, smem, hbm, hbm, hbm],
+        out_specs=(pl.BlockSpec(memory_space=pltpu.VMEM), hbm),
+        scratch_shapes=[
+            pltpu.VMEM((5, slots, slot_rows, share), bf16),
+            pltpu.VMEM((5, slots, slot_rows, share), bf16),
+            pltpu.SemaphoreType.DMA((5 * slots,)),
+            pltpu.SemaphoreType.DMA((5 * slots,)),
+            pltpu.SemaphoreType.DMA((7 * slots,)),
+            pltpu.SemaphoreType.DMA((7 * slots,)),
+            pltpu.SemaphoreType.DMA((31,)),
+            pltpu.SemaphoreType.DMA((31,)),
+            pltpu.SemaphoreType.DMA((slots + 2,)),
+        ],
+        compiler_params=pltpu.CompilerParams(
+            collective_id=0, has_side_effects=True, vmem_limit_bytes=24 * 2**20
+        ),
+        cost_estimate=pl.CostEstimate(flops=0, bytes_accessed=24 * 2**20, transcendentals=0),
+    )(bits, live, patches, qkv_w, out_w)
+
+
+def add_into(total, other, rows_at=16):
+    @pl.loop(0, total.shape[0] // rows_at)
+    def _(i):
+        at = pl.ds(pl.multiple_of(i * rows_at, rows_at), rows_at)
+        total[at, :] = (
+            total[at, :].astype(jnp.float32) + other[at, :].astype(jnp.float32)
+        ).astype(total.dtype)
+
+
+def reduce_kernel(
+    qkv_term, out_term, value_part, back_part,
+    grad_w, value_sum, back_sum,
+    mine, theirs, z_got, y_got, parts, x_got, l_got,
+    core_send, core_recv, z_send_sem, z_recv_sem, y_send, y_recv,
+    x_send, x_recv, l_send, l_recv, local_sem,
+):
+    z, yh, c, x, yl = coords()
+    qkv_cols, out_cols = qkv_term.shape[-1], out_term.shape[-1]
+    share = value_sum.shape[1]
+    z_up, z_down = lax.rem(z + 1, NZ), lax.rem(z + NZ - 1, NZ)
+    x_up, x_down = lax.rem(x + 1, NX), lax.rem(x + NX - 1, NX)
+    sibling = dev(z, yh, 1 - c, x, yl)
+    opposite = dev(z, 1 - yh, c, x, yl)
+    beside = dev(z, yh, c, x, 1 - yl)
+    up, down = dev(z_up, yh, c, x, yl), dev(z_down, yh, c, x, yl)
+    right, left = dev(z, yh, c, x_up, yl), dev(z, yh, c, x_down, yl)
+    greet([sibling, opposite, beside, up, down, right, left])
+    sent = []
+
+    def go(copy):
+        copy.start()
+        sent.append(copy)
+
+    core_sems, z_sems = (core_send, core_recv), (z_send_sem, z_recv_sem)
+    y_sems, x_sems, l_sems = (y_send, y_recv), (x_send, x_recv), (l_send, l_recv)
+    left_cols, right_cols = pl.ds(0, qkv_cols), pl.ds(qkv_cols, out_cols)
+
+    def z_at(distance):
+        return lax.rem(z + distance + NZ, NZ)
+
+    distances = [4, 3, -3, 2, -2, 1, -1, 0]
+    local = []
+    for i, distance in enumerate(distances):
+        zz = z_at(distance)
+        for j, (term, cols) in enumerate(((qkv_term, left_cols), (out_term, right_cols))):
+            go(
+                remote(
+                    term.at[zz, :, 1 - c], theirs.at[zz, :, :, cols], core_sems, i * 2 + j, sibling
+                )
+            )
+            copy = pltpu.make_async_copy(
+                term.at[zz, :, c], mine.at[zz, :, :, cols], local_sem.at[i * 2 + j]
+            )
+            copy.start()
+            local.append(copy)
+        if i == 0:
+            for p, part in enumerate((value_part, back_part)):
+                for shard in range(8):
+                    copy = pltpu.make_async_copy(
+                        part.at[:, pl.ds(shard * share, share)],
+                        parts.at[p, shard],
+                        local_sem.at[16 + p * 8 + shard],
+                    )
+                    copy.start()
+                    local.append(copy)
+    part_copies = local[2:18]
+    term_copies = local[:2] + local[18:]
+
+    def have(distance):
+        i = distances.index(distance)
+        zz = z_at(distance)
+        for j, (term, cols) in enumerate(((qkv_term, left_cols), (out_term, right_cols))):
+            term_copies[i * 2 + j].wait()
+            remote(
+                term.at[zz, :, c], theirs.at[zz, :, :, cols], core_sems, i * 2 + j, sibling
+            ).wait_recv()
+        for y in range(2):
+            add_into(mine.at[zz, y], theirs.at[zz, y])
+
+    def y_of(kind):
+        return yh if kind == 0 else 1 - yh
+
+    limits = {(0, 0): 4, (0, 1): 3, (1, 0): 3, (1, 1): 4}
+    z_slot = {}
+    for direction in range(2):
+        for kind in range(2):
+            for d in range(limits[direction, kind], 0, -1):
+                z_slot[direction, kind, d] = len(z_slot)
+
+    def z_go(direction, kind, d):
+        zz = z_at(d if direction == 0 else -d)
+        slot = z_slot[direction, kind, d]
+        go(
+            remote(
+                mine.at[zz, y_of(kind)], z_got.at[slot], z_sems, slot,
+                up if direction == 0 else down,
+            )
+        )
+
+    def z_take(direction, kind, d):
+        zz = z_at(d - 1 if direction == 0 else 1 - d)
+        slot = z_slot[direction, kind, d]
+        remote(mine.at[zz, y_of(kind)], z_got.at[slot], z_sems, slot, up).wait_recv()
+        add_into(mine.at[zz, y_of(kind)], z_got.at[slot])
+
+    x_limits = {(0, 0): 2, (0, 1): 1, (1, 0): 1, (1, 1): 2}
+    x_slot = {}
+    for p in range(2):
+        for direction in range(2):
+            for kind in range(2):
+                for d in range(x_limits[direction, kind], 0, -1):
+                    x_slot[p, direction, kind, d] = len(x_slot)
+
+    def x_shard(direction, kind, d):
+        xx = lax.rem(x + (d if direction == 0 else NX - d), NX)
+        return xx * 2 + (yl if kind == 0 else 1 - yl)
+
+    def x_go(p, direction, kind, d):
+        slot = x_slot[p, direction, kind, d]
+        go(
+            remote(
+                parts.at[p, x_shard(direction, kind, d)], x_got.at[slot], x_sems, slot,
+                right if direction == 0 else left,
+            )
+        )
+
+    def x_take(p, direction, kind, d):
+        slot = x_slot[p, direction, kind, d]
+        shard = x_shard(direction, kind, d - 1)
+        remote(parts.at[p, shard], x_got.at[slot], x_sems, slot, right).wait_recv()
+        add_into(parts.at[p, shard], x_got.at[slot])
+
+    def x_first(p):
+        for shard in range(8):
+            part_copies[p * 8 + shard].wait()
+        for d in (2, 1):
+            for kind in (1, 0):
+                for direction in range(2):
+                    if d == x_limits[direction, kind]:
+                        x_go(p, direction, kind, d)
+
+    def x_second(p):
+        x_take(p, 1, 1, 2)
+        x_go(p, 1, 1, 1)
+        x_take(p, 0, 0, 2)
+        x_go(p, 0, 0, 1)
+
+    def x_third(p):
+        x_take(p, 0, 1, 1)
+        x_take(p, 1, 1, 1)
+        go(remote(parts.at[p, x * 2 + 1 - yl], l_got.at[p], l_sems, p, beside))
+        x_take(p, 1, 0, 1)
+        x_take(p, 0, 0, 1)
+
+    def x_last(p, out):
+        remote(parts.at[p, x * 2 + yl], l_got.at[p], l_sems, p, beside).wait_recv()
+
+        @pl.loop(0, out.shape[0] // 16)
+        def _(i):
+            at = pl.ds(pl.multiple_of(i * 16, 16), 16)
+            out[at, :] = parts[p, x * 2 + yl, at, :].astype(jnp.float32) + l_got[
+                p, at, :
+            ].astype(jnp.float32)
+
+    x_first(0)
+    have(4)
+    z_go(1, 1, 4)
+    z_go(0, 0, 4)
+    have(3)
+    z_go(0, 1, 3)
+    have(-3)
+    z_go(1, 0, 3)
+    x_first(1)
+    have(2)
+    have(-2)
+    x_second(0)
+    z_take(1, 1, 4)
+    z_go(1, 1, 3)
+    z_take(0, 0, 4)
+    z_go(0, 0, 3)
+    z_take(0, 1, 3)
+    z_go(0, 1, 2)
+    z_take(1, 0, 3)
+    z_go(1, 0, 2)
+    x_third(0)
+    have(1)
+    have(-1)
+    have(0)
+    z_take(1, 1, 3)
+    z_go(1, 1, 2)
+    z_take(0, 0, 3)
+    z_go(0, 0, 2)
+    x_second(1)
+    z_take(0, 1, 2)
+    z_go(0, 1, 1)
+    z_take(1, 0, 2)
+    z_go(1, 0, 1)
+    x_last(0, value_sum)
+    z_take(1, 1, 2)
+    z_go(1, 1, 1)
+    z_take(0, 0, 2)
+    z_go(0, 0, 1)
+    x_third(1)
+    z_take(0, 1, 1)
+    z_take(1, 1, 1)
+    go(remote(mine.at[z, 1 - yh], y_got, y_sems, 0, opposite))
+    z_take(1, 0, 1)
+    z_take(0, 0, 1)
+    x_last(1, back_sum)
+    remote(mine.at[z, yh], y_got, y_sems, 0, opposite).wait_recv()
+
+    @pl.loop(0, grad_w.shape[0] // 16)
+    def _(i):
+        at = pl.ds(pl.multiple_of(i * 16, 16), 16)
+        grad_w[at, :] = mine[z, yh, at, :].astype(jnp.float32) + y_got[at, :].astype(jnp.float32)
+
+    for copy in sent:
+        copy.wait_send()
+
+
+def reduce(qkv_term, out_term, value_part, back_part):
+    bf16, f32 = jnp.bfloat16, jnp.float32
+    model, qkv_cols = qkv_term.shape
+    out_cols = out_term.shape[1]
+    wide = qkv_cols + out_cols
+    depth = model // 32
+    tok = value_part.shape[0]
+    share = model // 8
+    hbm = pl.BlockSpec(memory_space=pl.ANY)
+    vmem = pl.BlockSpec(memory_space=pltpu.VMEM)
+    dma = pltpu.SemaphoreType.DMA
+    return pl.pallas_call(
+        reduce_kernel,
+        out_shape=(
+            jax.ShapeDtypeStruct((depth, wide), f32),
+            jax.ShapeDtypeStruct((tok, share), f32),
+            jax.ShapeDtypeStruct((tok, share), f32),
+        ),
+        in_specs=[hbm] * 4,
+        out_specs=(vmem,) * 3,
+        scratch_shapes=[
+            pltpu.VMEM((NZ, 2, depth, wide), bf16),
+            pltpu.VMEM((NZ, 2, depth, wide), bf16),
+            pltpu.VMEM((14, depth, wide), bf16),
+            pltpu.VMEM((depth, wide), bf16),
+            pltpu.VMEM((2, 8, tok, share), bf16),
+            pltpu.VMEM((12, tok, share), bf16),
+            pltpu.VMEM((2, tok, share), bf16),
+            dma((16,)), dma((16,)), dma((14,)), dma((14,)), dma((1,)), dma((1,)),
+            dma((12,)), dma((12,)), dma((2,)), dma((2,)), dma((32,)),
+        ],
+        compiler_params=pltpu.CompilerParams(
+            collective_id=1, has_side_effects=True, vmem_limit_bytes=40 * 2**20
+        ),
+        cost_estimate=pl.CostEstimate(flops=0, bytes_accessed=30 * 2**20, transcendentals=0),
+    )(
+        qkv_term.reshape(NZ, 2, 2, depth, qkv_cols),
+        out_term.reshape(NZ, 2, 2, depth, out_cols),
+        value_part,
+        back_part,
+    )
 
 
 def norm_rows(values):
@@ -41,15 +547,10 @@
     qkv_cols = qkv_weight.shape[1]
     out_cols = out_weight.shape[1]
     local_heads = out_cols // head_dim
-    row_slot = jnp.arange(tok_rows, dtype=jnp.int32) // slot_rows
-    holding = lax.dynamic_slice_in_dim(patches, my_group * share_width, share_width, 1)
-    digit_count = replicas.bit_length() - 1
-    digit_order = list(range(digit_count))
-    for bit_place in digit_order:
-        partner = partner_2(holding, "fsdp", bit_place)
-        moving = jnp.bitwise_and(jnp.right_shift(masks, bit_place), 1) == 1
-        take_rows = jnp.take(moving, row_slot)
-        holding = jnp.where(take_rows[:, None], partner, holding)
+    bit = [jnp.bitwise_and(jnp.right_shift(masks, place), 1) for place in range(5)]
+    bits = jnp.stack(
+        [bit[1], bit[4], bit[3] ^ bit[4], bit[2] ^ bit[3], bit[0]], axis=1
+    ).astype(jnp.int32)
     replica_ids = jnp.arange(replicas, dtype=jnp.int32)
     sources = jnp.bitwise_xor(my_replica, masks)
     run_counts = jnp.sum(jnp.where(replica_ids[:, None] == sources[None, :], counts, 0), axis=0)
@@ -57,12 +558,11 @@
     live_slots = places[None, :] < run_counts[:, None]
     is_live = live_slots.reshape(tok_rows)
     allowed = live_slots[:, :, None] & live_slots[:, None, :] | jnp.eye(slot_rows, dtype=bool)[None]
-    packed = jnp.where(is_live[:, None], holding, jnp.zeros((), holding.dtype))
-    block_rows = lax.all_gather(packed, "tp", axis=1, tiled=True)
-    qkv_full, out_full = (
-        lax.all_gather(qkv_weight, "fsdp", axis=0, tiled=True),
-        lax.all_gather(out_weight, "fsdp", axis=0, tiled=True),
-    )
+    block_rows, weights = gather(
+        bits, run_counts.astype(jnp.int32), patches, qkv_weight, out_weight
+    )
+    weights = weights.reshape(model_width, qkv_cols + out_cols)
+    qkv_full, out_full = weights[:, :qkv_cols], weights[:, qkv_cols:]
     centred_rows, row_factor = norm_rows(block_rows.astype(jnp.float32))
     normed = (centred_rows * norm_gain).astype(jnp.bfloat16)
     projected = jnp.dot(normed, qkv_full, preferred_element_type=jnp.float32).reshape(
@@ -86,10 +586,6 @@
     partial_value = lax.dot_general(
         mixed, out_full, (((1,), (1,)), ((), ())), preferred_element_type=jnp.float32
     )
-    attended = lax.psum_scatter(
-        partial_value.astype(jnp.bfloat16), "tp", scatter_dimension=1, tiled=True
-    ).astype(jnp.float32)
-    attended = jnp.where(is_live[:, None], attended, 0.0).astype(jnp.bfloat16)
     upstream_rows = jnp.where(is_live[:, None], cotangent, jnp.zeros((), cotangent.dtype))
     grad_mixed = jnp.dot(upstream_rows, out_full, preferred_element_type=jnp.float32).astype(
         jnp.bfloat16
@@ -122,22 +618,29 @@
     out_term = lax.dot_general(
         upstream_rows, mixed, (((0,), (0,)), ((), ())), preferred_element_type=jnp.float32
     )
-    stacked = lax.psum_scatter(
-        jnp.concatenate([qkv_term, out_term], axis=1).astype(jnp.bfloat16),
-        "fsdp",
-        scatter_dimension=0,
-        tiled=True,
-    ).astype(jnp.float32)
-    grad_qkv_weight = stacked[:, :qkv_cols]
-    grad_out_weight = stacked[:, qkv_cols:]
     partial_back = lax.dot_general(
         grad_qkv, qkv_full, (((1,), (1,)), ((), ())), preferred_element_type=jnp.float32
     )
-    summed = lax.psum(partial_back.astype(jnp.bfloat16), "tp").astype(jnp.float32)
-    grad_full = norm_back(summed * norm_gain, centred_rows, row_factor)
-    grad_share = lax.dynamic_slice_in_dim(grad_full, my_group * share_width, share_width, 1)
-    grad_rows = grad_share.astype(jnp.bfloat16)
-    return (attended, grad_rows, grad_qkv_weight, grad_out_weight)
+    partial_back = partial_back.astype(jnp.bfloat16)
+    scaled = partial_back.astype(jnp.float32) * norm_gain
+    sums = jnp.stack([jnp.sum(scaled, -1), jnp.sum(scaled * centred_rows, -1)])
+    sums = lax.psum(sums, "tp") / model_width
+    grad_w, value_sum, back_sum = reduce(
+        qkv_term.astype(jnp.bfloat16),
+        out_term.astype(jnp.bfloat16),
+        partial_value.astype(jnp.bfloat16),
+        partial_back,
+    )
+    attended = jnp.where(is_live[:, None], value_sum, 0.0).astype(jnp.bfloat16)
+    gain_share = lax.dynamic_slice_in_dim(norm_gain, my_group * share_width, share_width, 0)
+    centred_share = lax.dynamic_slice_in_dim(
+        centred_rows, my_group * share_width, share_width, 1
+    )
+    grad_rows = row_factor * (
+        back_sum * gain_share - sums[0][:, None] - centred_share * sums[1][:, None]
+    )
+    grad_rows = grad_rows.astype(jnp.bfloat16)
+    return (attended, grad_rows, grad_w[:, :qkv_cols], grad_w[:, qkv_cols:])
 
 
 def solution(mesh):

time: 704 us -> 289 us (0.41)
  waiting for transfers between devices: 537 us -> 0 us
  Pallas kernels: 0 us -> 176 us
  other arithmetic: 44.1 us -> 15.4 us
  blocking collectives: 0 us -> 16.8 us
  local copies, waits for them, and re-layouts: 45.4 us -> 29.4 us
  starting transfers between devices: 14.4 us -> 0 us
  between operations: 14.5 us -> 1 us
    unnamed x8 -> x0, waiting for transfers between devices: 236 us -> none
    all_gather x3 -> x0, waiting for transfers between devices: 178 us -> none  [the longest x1 96.7 us: per_device(): lax.all_gather(qkv_weight, 'fsdp', axis=0, tiled=True)]
    pallas_call x0 -> x2, Pallas kernels: none -> 176 us  [the longest x1 104 us: gather(): pl.pallas_call(gather_kernel, out_shape=(jax.ShapeDtypeStruct((tok, model...]
    psum x1 -> x0, waiting for transfers between devices: 85.1 us -> none  [per_device(): lax.psum(partial_back.astype(jnp.bfloat16), 'tp').astype(jnp.float32)]
    ppermute x5 -> x0, waiting for transfers between devices: 37.9 us -> none  [partner_2(): return lax.ppermute(value, axis, pairs)]
    psum x0 -> x1, blocking collectives: none -> 16.8 us  [per_device(): sums = lax.psum(sums, 'tp') / model_width]
    unnamed x34 -> x39, local copies, waits for them, and re-layouts: 27 us -> 11 us
    select_n x10 -> x0, other arithmetic: 15.4 us -> none  [the longest x5 12.9 us: per_device(): take_rows = jnp.take(moving, row_slot)]
  transfers between devices with their start and end apart: 11 -> 0, of which waited for: 10 -> 0; matrix products, arithmetic and copies ran while one was open for 11% -> 0% of each run, Pallas kernels for 0% -> 0%
where the time goes in v1:
time: 289 us; the launch traced here: 286 us
  Pallas kernels  176 us (61%)
  matrix products  47.7 us (17%)
  local copies, waits for them, and re-layouts  29.4 us (10%)
  blocking collectives  16.8 us (6%)
  other arithmetic  15.4 us (5%)
    pallas_call x1, Pallas kernels, gather(): pl.pallas_call(gather_kernel, out_shape=(jax.ShapeDtypeStruct((tok, model...  104 us
    pallas_call x1, Pallas kernels, reduce(): pl.pallas_call(reduce_kernel, out_shape=(jax.ShapeDtypeStruct((depth, wid...  72.1 us
    psum x1, blocking collectives, per_device(): sums = lax.psum(sums, 'tp') / model_width  16.8 us
    dot_general x1, matrix products, per_device(): lax.dot_general(grad_qkv, qkv_full, (((1,), (1,)), ((), ())), preferred_e...  11.6 us
    unnamed x39, local copies, waits for them, and re-layouts  11 us
    dot_general x1, matrix products, per_device(): lax.dot_general(normed, grad_qkv, (((0,), (0,)), ((), ())), preferred_ele...  6.94 us

profile of v1, /device:TPU:2, one launch (start us, length us, event | category | flops | bytes accessed | tf_op | source)
XLA Modules:
  0.0 286.2 jit_solution(1951625080474516524)
XLA Ops:
  0.6 0.0 copy-start.14
  0.6 0.7 broadcast_xor_fusion
  1.3 0.1 copy.24
  1.4 0.1 copy.25
  1.5 0.1 copy.26
  1.6 0.1 copy.27
  1.7 0.1 copy.28
  1.8 0.1 stack.48.bits_ref
  1.9 0.9 select_reduce_fusion.live_ref
  2.7 1.8 copy-done.1
  4.5 0.9 copy-done.2
  5.5 0.9 copy-done.3
  6.3 103.8 %shard_map.111 = (bf16[448,3072]{1,0:T(8,128)(2,1)S(1)}, bf16[32,96,1536]{2,1,0:T(8,128)(2,1)S(1)}) custom-call(s32[4,5]{1,0:T(4,128)S(1)} %stack.48.bits_ref, s32[4]{0:T(128)S(1)} %select_reduce_fusion.live_ref, bf16[448,3072]{1,0:T(8,128)(2,1)S(1)} %copy-done.1, bf16[96,1152]{1,0:T(8,128)(2,1)S(1)} %copy-done.2, bf16[96,384]{1,0:T(8,128)(2,1)S(1)} %copy-done.3), custom_call_target="tpu_custom_call" | custom-call | bytes 25165824 | tf_op jit(solution)/shard_map/pallas_call | solution.py:232
  110.2 0.0 copy-start.4
  110.2 0.4 convert_reduce_fusion
  110.6 0.9 fusion.6
  111.5 2.3 copy-done.4
  113.8 0.0 copy-done.14
  113.8 5.7 %fusion.4 = f32[448,1152]{0,1:T(8,128)} fusion(bf16[3072,1536]{1,0:T(8,128)(2,1)S(1)} %bitcast.93, f32[3072]{0:T(1024)S(1)} %copy-done.14, bf16[448,3072]{1,0:T(8,128)(2,1)S(1)} %get-tuple-element.9, f32[448]{0:T(512)S(1)} %add_rsqrt_fusion.2, f32[448]{0:T(512)S(1)} %broadcast_multiply_fusion.7), kind=kOutput, calls=%fused_computation.7 | convolution fusion | flops 3177775104 | bytes 11911168 | tf_op jit(solution)/shard_map/dot_general | solution.py:568
  119.4 4.0 %reshape.156 = f32[4,112,3,3,128]{1,0,4,3,2:T(4,128)} reshape(f32[448,1152]{0,1:T(8,128)} %fusion.4) | data formatting | bytes 4128768 | tf_op jit(solution)/shard_map/reshape | solution.py:568
  123.5 3.0 %fusion.44 = (f32[4,112,3]{1,0,2:T(4,128)S(1)}, f32[4,112,3,1,128]{1,0,4,3,2:T(4,128)}, f32[4,112,3]{1,0,2:T(4,128)S(1)}, f32[4,112,3,1,128]{1,0,4,3,2:T(4,128)}) fusion(f32[4,112,3,3,128]{1,0,4,3,2:T(4,128)} %reshape.156), kind=kLoop, calls=%fused_computation.93 | loop fusion | flops 341376 | bytes 2763264 | tf_op jit(solution)/shard_map/reduce_sum | solution.py:522
  126.5 1.4 copy.46
  127.9 0.0 copy-start.5
  127.9 0.5 multiply_reduce_fusion.5
  128.4 0.4 copy-done.5
  128.8 1.4 copy.47
  130.2 0.5 multiply_reduce_fusion.4
  130.7 2.0 slice.49
  132.7 1.9 copy.48
  134.7 0.1 iota_compare_fusion.2
  134.7 0.1 lt.35
  134.8 4.9 %fusion.17 = bf16[448,384]{1,0:T(8,128)(2,1)} fusion(bf16[3072,1536]{1,0:T(8,128)(2,1)} %bitcast.94, bf16[448,3072]{1,0:T(8,128)(2,1)} %param.9, pred[448]{0:T(512)(128)(4,1)S(1)} %lt.35), kind=kOutput, calls=%fused_computation.27 | convolution fusion | flops 1058512896 | bytes 5456320 | tf_op jit(solution)/shard_map/dot_general | solution.py:590
  139.7 2.0 reshape.161
  141.7 2.3 fusion.27
  144.0 0.1 and_or_fusion
  144.2 3.1 %multiply_reduce_fusion.3 = (f32[4,3,112]{2,1,0:T(4,128)S(1)}, f32[4,3,112,112]{2,3,1,0:T(8,128)}) fusion(f32[4,3,112,112]{2,3,1,0:T(8,128)} %fusion.27, pred[4,112,112]{1,2,0:T(8,128)(4,1)S(1)} %and_or_fusion, f32[4,112,3,1,128]{4,1,2,0,3:T(8,128)S(1)} %copy.47, f32[128]{0:T(128)S(1)} %get-tuple-element.30, f32[4,112,3]{1,2,0:T(4,128)S(1)} %get-tuple-element.42, ...), kind=kOutput, calls=%fused_computation.42 | convolution fusion | flops 40513648 | bytes 2658560 | tf_op jit(solution)/shard_map/div | solution.py:580
  147.3 1.5 multiply_convert_fusion.6
  148.9 2.6 fusion.42
  151.5 1.9 fusion.24
  153.4 2.0 fusion.43
  155.4 0.0 copy-start.15
  155.4 0.9 fusion.25
  156.3 0.3 fusion.21
  156.7 1.1 pad_maximum_fusion
  157.8 3.3 %copy.37 = bf16[4,112,3,3,128]{1,0,4,3,2:T(4,128)(2,1)} copy(bf16[4,112,3,3,128]{4,1,2,0,3:T(8,128)(2,1)} %pad_maximum_fusion) | data formatting | bytes 2064384 | tf_op jit(solution)/shard_map/stack | solution.py:611
  161.0 3.3 %convert_element_type.65 = bf16[448,1152]{0,1:T(8,128)(2,1)} reshape(bf16[4,112,3,3,128]{1,0,4,3,2:T(4,128)(2,1)} %copy.37) | data formatting | bytes 2064384 | tf_op jit(solution)/shard_map/convert_element_type | solution.py:612
  164.4 11.6 %fusion.7 = (f32[448]{0:T(512)S(1)}, f32[448]{0:T(512)S(1)}, f32[448,3072]{1,0:T(8,128)}, bf16[448,3072]{1,0:T(8,128)(2,1)}) fusion(f32[3072]{0:T(1024)S(1)} %copy-done.15, f32[448]{0:T(512)S(1)} %add_rsqrt_fusion.2, f32[448]{0:T(512)S(1)} %broadcast_multiply_fusion.7, bf16[448,3072]{1,0:T(8,128)(2,1)S(1)} %get-tuple-element.9, ...), kind=kOutput, calls=%fused_computation.12 | convolution fusion | flops 3183279104 | bytes 19287040 | tf_op jit(solution)/shard_map/dot_general | solution.py:621
  176.0 16.8 %psum.7 = f32[2,448]{1,0:T(2,128)S(1)} all-reduce(f32[2,448]{1,0:T(2,128)S(1)} %pad_maximum_fusion.1), channel_id=1, replica_groups=mesh['fsdp'=32,'tp'=8] {'tp'}, use_global_device_ids=true, to_apply=%region_15.16 | all-reduce | flops 896 | bytes 7168 | tf_op jit(solution)/shard_map/psum | solution.py:627
  192.8 2.0 fusion.20
  194.9 1.2 copy.39
  196.1 0.3 reshape.159
  196.4 0.0 copy-start.17
  196.4 3.5 %convolution_convert_fusion.1.value_part = bf16[448,3072]{1,0:T(8,128)(2,1)S(1)} fusion(bf16[448,384]{0,1:T(8,128)(2,1)S(1)} %reshape.159, bf16[3072,1536]{1,0:T(8,128)(2,1)} %bitcast.96), kind=kOutput, calls=%fused_computation.15 | convolution fusion | flops 1058340864 | bytes 5455872 | tf_op jit(solution)/shard_map/dot_general | solution.py:586
  199.8 0.0 copy-done.17
  199.8 0.0 copy-start.10
  199.9 0.0 copy-start.16
  199.9 2.8 convolution_convert_fusion.2
  202.7 6.9 %convolution_convert_fusion = bf16[3072,1152]{1,0:T(8,128)(2,1)} fusion(bf16[448,1152]{0,1:T(8,128)(2,1)S(1)} %copy-done.10, f32[3072]{0:T(1024)S(1)} %copy-done.16, bf16[448,3072]{1,0:T(8,128)(2,1)S(1)} %get-tuple-element.9, f32[448]{0:T(512)S(1)} %add_rsqrt_fusion.2, f32[448]{0:T(512)S(1)} %broadcast_multiply_fusion.7), kind=kOutput, calls=%fused_computation | convolution fusion | flops 3181314048 | bytes 10878464 | tf_op jit(solution)/shard_map/dot_general | solution.py:615
  209.6 72.1 %shard_map.112 = (f32[96,1536]{1,0:T(8,128)S(1)}, f32[448,384]{1,0:T(8,128)S(1)}, f32[448,384]{1,0:T(8,128)S(1)}) custom-call(bf16[8,2,2,96,1152]{4,3,2,1,0:T(8,128)(2,1)} %bitcast.97, bf16[8,2,2,96,384]{4,3,2,1,0:T(8,128)(2,1)S(1)} %bitcast.92, bf16[448,3072]{1,0:T(8,128)(2,1)S(1)} %convolution_convert_fusion.1.value_part, bf16[448,3072]{1,0:T(8,128)(2,1)S(1)} %copy-done), custom_call_target="tpu_custom_call" | custom-call | bytes 31457280 | tf_op jit(solution)/shard_map/pallas_call | solution.py:489
  281.7 0.1 dynamic_slice.6
  281.8 2.1 multiply_convert_fusion.3
  283.9 0.8 slice.43
  284.7 0.9 select_convert_fusion
  285.5 0.7 slice.44
  (36 shorter events, 0.1 us)
Async XLA Ops:
  0.6 113.2 %copy-start.14 = (f32[3072]{0:T(1024)S(1)}, f32[3072]{0:T(1024)}, u32[]{:S(2)}) copy-start(f32[3072]{0:T(1024)} %param.12) | copy-start | bytes 36868
  2.7 1.8 copy-start.1
  4.5 0.9 copy-start.2
  5.5 0.9 copy-start.3
  110.2 3.6 %copy-start.4 = (bf16[32,96,1536]{2,1,0:T(8,128)(2,1)}, bf16[32,96,1536]{2,1,0:T(8,128)(2,1)S(1)}, u32[]{:S(2)}) copy-start(bf16[32,96,1536]{2,1,0:T(8,128)(2,1)S(1)} %get-tuple-element.10) | copy-start | bytes 28311556
  127.9 0.9 copy-start.5
  134.8 4.9 %copy-start.12 = (pred[448]{0:T(512)(128)(4,1)}, pred[448]{0:T(512)(128)(4,1)S(1)}, u32[]{:S(2)}) copy-start(pred[448]{0:T(512)(128)(4,1)S(1)} %lt.35) | copy-start | bytes 1348
  134.8 9.3 %copy-start.11 = (f32[2,128]{1,0:T(2,128)S(1)}, f32[2,128]{1,0:T(2,128)}, u32[]{:S(2)}) copy-start(f32[2,128]{1,0:T(2,128)} %param.13) | copy-start | bytes 3076
  147.3 6.1 %copy-start.6 = (f32[4,112,3,1,128]{4,1,2,0,3:T(8,128)S(1)}, f32[4,112,3,1,128]{4,1,2,0,3:T(8,128)}, u32[]{:S(2)}) copy-start(f32[4,112,3,1,128]{4,1,2,0,3:T(8,128)} %copy-done.5) | copy-start | bytes 2064388
  147.3 9.0 %copy-start.7 = (f32[4,3,112,112]{2,3,1,0:T(8,128)S(1)}, f32[4,3,112,112]{2,3,1,0:T(8,128)}, u32[]{:S(2)}) copy-start(f32[4,3,112,112]{2,3,1,0:T(8,128)} %get-tuple-element.38) | copy-start | bytes 1806340
  147.3 9.0 %copy-start.9 = (bf16[4,112,3,128]{3,2,1,0:T(4,128)(2,1)S(1)}, bf16[4,112,3,128]{3,2,1,0:T(4,128)(2,1)}, u32[]{:S(2)}) copy-start(bf16[4,112,3,128]{3,2,1,0:T(4,128)(2,1)} %reshape.161) | copy-start | bytes 1032196
  155.4 9.0 %copy-start.15 = (f32[3072]{0:T(1024)S(1)}, f32[3072]{0:T(1024)}, u32[]{:S(2)}) copy-start(f32[3072]{0:T(1024)} %param.12) | copy-start | bytes 36868
  164.4 28.5 %copy-start.8 = (f32[4,3,112,112]{2,3,1,0:T(8,128)S(1)}, f32[4,3,112,112]{2,3,1,0:T(8,128)}, u32[]{:S(2)}) copy-start(f32[4,3,112,112]{2,3,1,0:T(8,128)} %get-tuple-element.38) | copy-start | bytes 1806340
  196.4 3.5 %copy-start.17 = (bf16[448,3072]{1,0:T(8,128)(2,1)S(1)}, bf16[448,3072]{1,0:T(8,128)(2,1)}, u32[]{:S(2)}) copy-start(bf16[448,3072]{1,0:T(8,128)(2,1)} %param.9) | copy-start | bytes 8257540
  199.8 2.8 copy-start.10
  199.9 2.8 copy-start.16
  202.7 7.0 %copy-start = (bf16[448,3072]{1,0:T(8,128)(2,1)S(1)}, bf16[448,3072]{1,0:T(8,128)(2,1)}, u32[]{:S(2)}) copy-start(bf16[448,3072]{1,0:T(8,128)(2,1)} %get-tuple-element.41.back_part) | copy-start | bytes 8257540
  209.6 75.0 %copy-start.13 = (pred[448]{0:T(512)(128)(4,1)S(1)}, pred[448]{0:T(512)(128)(4,1)}, u32[]{:S(2)}) copy-start(pred[448]{0:T(512)(128)(4,1)} %copy-done.12) | copy-start | bytes 1348

commit v2 on v1

v2 whole, which is shorter than its diff:
```python
import functools
import jax
import jax.numpy as jnp
from jax import lax
from jax.experimental import pallas as pl
from jax.experimental.pallas import tpu as pltpu
from jax.sharding import PartitionSpec as P

MESH = pl.DeviceIdType.MESH
epsilon = 1e-06
NZ, NX = 8, 4


def coords():
    f = lax.axis_index("fsdp")
    t = lax.axis_index("tp")
    z, yh, c = lax.div(f, 4), lax.rem(lax.div(f, 2), 2), lax.rem(f, 2)
    x, yl = lax.div(t, 2), lax.rem(t, 2)
    return z, yh, c, x, yl


def dev(z, yh, c, x, yl):
    return (z * 4 + yh * 2 + c, x * 2 + yl)


def remote(src, dst, sems, slot, target):
    send, recv = sems
    return pltpu.make_async_remote_copy(
        src_ref=src,
        dst_ref=dst,
        send_sem=send.at[slot],
        recv_sem=recv.at[slot],
        device_id=target,
        device_id_type=MESH,
    )


def greet(partners):
    barrier = pltpu.get_barrier_semaphore()
    for partner in partners:
        pl.semaphore_signal(barrier, inc=1, device_id=partner, device_id_type=MESH)
    pl.semaphore_wait(barrier, len(partners))


def gather_kernel(
    bits_ref, live_ref, patches, qkv_w, out_w, rows, weights,
    hold, got, a_send, a_recv, b_send, b_recv, c_send, c_recv, local_sem,
):
    z, yh, c, x, yl = coords()
    me = dev(z, yh, c, x, yl)
    f, t = me
    slots, slot_rows, share = hold.shape[1], hold.shape[2], hold.shape[3]
    qkv_cols = qkv_w.shape[1]
    z_up, z_down = lax.rem(z + 1, NZ), lax.rem(z + NZ - 1, NZ)
    x_up, x_down = lax.rem(x + 1, NX), lax.rem(x + NX - 1, NX)
    low4, low2 = lax.rem(z, 4), lax.rem(z, 2)
    across = dev(z, 1 - yh, c, x, 1 - yl)
    z7 = dev(7 - z, yh, c, x, yl)
    z3 = dev(z + 3 - 2 * low4, yh, c, x, yl)
    z1 = dev(z + 1 - 2 * low2, yh, c, x, yl)
    sibling = dev(z, yh, 1 - c, x, yl)
    opposite = dev(z, 1 - yh, c, x, yl)
    beside = dev(z, yh, c, x, 1 - yl)
    up, down = dev(z_up, yh, c, x, yl), dev(z_down, yh, c, x, yl)
    right, left = dev(z, yh, c, x_up, yl), dev(z, yh, c, x_down, yl)
    greet([across, z7, z3, z1, sibling, opposite, beside, up, down, right, left])

    sent = []

    def go(copy):
        copy.start()
        sent.append(copy)

    a_sems, b_sems, c_sems = (a_send, a_recv), (b_send, b_recv), (c_send, c_recv)

    def columns(index):
        return pl.ds(pl.multiple_of(index * share, 128), share)

    def slot_at(k):
        return pl.ds(k * slot_rows, slot_rows)

    for k in range(slots):
        go(remote(patches.at[slot_at(k), columns(x * 2 + 1 - yl)], got.at[0, k], a_sems, k, across))
    own = [
        pltpu.make_async_copy(patches.at[slot_at(k), columns(t)], hold.at[0, k], local_sem.at[k])
        for k in range(slots)
    ]
    own_w = [
        pltpu.make_async_copy(qkv_w, weights.at[f, :, pl.ds(0, qkv_cols)], local_sem.at[slots]),
        pltpu.make_async_copy(
            out_w, weights.at[f, :, pl.ds(qkv_cols, weights.shape[2] - qkv_cols)],
            local_sem.at[slots + 1],
        ),
    ]
    for copy in own_w + own:
        copy.start()
    for copy in own_w:
        copy.wait()

    def weight_copy(piece, slot, target):
        return remote(weights.at[piece], weights.at[piece], c_sems, slot, target)

    def fid(zz, kind):
        return zz * 4 + (yh if kind == 0 else 1 - yh) * 2 + c

    def sib_id(zz, kind):
        return zz * 4 + (yh if kind == 0 else 1 - yh) * 2 + 1 - c

    limits = {(0, 0): 4, (0, 1): 3, (1, 0): 3, (1, 1): 4}
    z_slot = {}
    for direction in range(2):
        for kind in range(2):
            for d in range(1, limits[direction, kind] + 1):
                z_slot[direction, kind, d] = 1 + len(z_slot)
    pieces = [(0, 0), (0, 1)]
    core_slot = {}

    def core_index(key):
        if key not in core_slot:
            core_slot[key] = 15 + len(core_slot)
        return core_slot[key]

    def z_at(distance):
        return lax.rem(z + distance + NZ, NZ)

    def share_core(distance, kind):
        go(weight_copy(fid(z_at(distance), kind), core_index((distance, kind)), sibling))

    def z_send(direction, kind, distance_travelled):
        source = z_at(-distance_travelled if direction == 0 else distance_travelled)
        go(
            weight_copy(
                fid(source, kind), z_slot[direction, kind, distance_travelled + 1],
                up if direction == 0 else down,
            )
        )

    def z_receive(direction, kind, d):
        signed = -d if direction == 0 else d
        weight_copy(fid(z_at(signed), kind), z_slot[direction, kind, d], up).wait_recv()
        if d < limits[direction, kind]:
            z_send(direction, kind, d)
        share_core(signed, kind)

    go(weight_copy(f, 0, opposite))
    share_core(0, 0)

    for copy in own:
        copy.wait()

    partner = {3: z3, 7: z7, 1: z1, 0: sibling}
    column = {7: 1, 3: 2, 1: 3, 0: 4}
    order = [[7, 3, 1, 0], [3, 7, 1, 0], [7, 3, 1, 0], [3, 7, 1, 0]]

    def merge(k, step, bit_column):
        remote(got.at[step, k], got.at[step, k], a_sems, step * slots + k, sibling).wait_recv()
        taken = bits_ref[k, bit_column] > 0
        return lax.select_n(taken, hold[step, k], got[step, k])

    for step in range(4):
        for k in range(slots):
            which = order[k][step]
            before = 0 if step == 0 else column[order[k][step - 1]]
            hold[step + 1, k] = merge(k, step, before)
            go(
                remote(
                    hold.at[step + 1, k], got.at[step + 1, k], a_sems,
                    (step + 1) * slots + k, partner[which],
                )
            )
        if step == 0:
            z_send(0, 0, 0)
            z_send(1, 0, 0)
            weight_copy(fid(z, 1), 0, opposite).wait_recv()
            z_send(0, 1, 0)
            z_send(1, 1, 0)
            share_core(0, 1)

    def row_copy(k, xx, y_low, which, target):
        view = rows.at[slot_at(k), columns(xx * 2 + y_low)]
        return remote(view, view, b_sems, k * 7 + which, target)

    for k in range(slots):
        merged = merge(k, 4, column[order[k][3]]).astype(jnp.float32)
        place = lax.broadcasted_iota(jnp.int32, (slot_rows, share), 0)
        live = place < live_ref[k]
        rows[slot_at(k), columns(t)] = jnp.where(live, merged, 0.0).astype(rows.dtype)
        go(row_copy(k, x, yl, 0, beside))
        go(row_copy(k, x, yl, 1, right))
        go(row_copy(k, x, yl, 4, left))

    def rows_second(k):
        row_copy(k, x, 1 - yl, 0, beside).wait_recv()
        go(row_copy(k, x, 1 - yl, 3, right))
        go(row_copy(k, x, 1 - yl, 5, left))

    def rows_third(k):
        row_copy(k, x_down, yl, 1, right).wait_recv()
        go(row_copy(k, x_down, yl, 2, right))
        row_copy(k, x_up, 1 - yl, 5, left).wait_recv()
        go(row_copy(k, x_up, 1 - yl, 6, left))

    for d in range(1, 5):
        for kind in range(2):
            for direction in range(2):
                if d <= limits[direction, kind]:
                    z_receive(direction, kind, d)
        if d == 1:
            for k in range(slots):
                rows_second(k)
                rows_third(k)
    for k in range(slots):
        row_copy(k, lax.rem(x + 2, NX), yl, 2, right).wait_recv()
        row_copy(k, x_down, 1 - yl, 3, right).wait_recv()
        row_copy(k, x_up, yl, 4, left).wait_recv()
        row_copy(k, lax.rem(x + 2, NX), 1 - yl, 6, left).wait_recv()
    for (distance, kind), slot in core_slot.items():
        weight_copy(sib_id(z_at(distance), kind), slot, sibling).wait_recv()
    for copy in sent:
        copy.wait_send()


def gather(bits, live, patches, qkv_w, out_w):
    tok, model = patches.shape
    slots = bits.shape[0]
    share = model // 8
    slot_rows = tok // slots
    bf16 = jnp.bfloat16
    depth, wide = qkv_w.shape[0], qkv_w.shape[1] + out_w.shape[1]
    hbm = pl.BlockSpec(memory_space=pl.ANY)
    smem = pl.BlockSpec(memory_space=pltpu.SMEM)
    return pl.pallas_call(
        gather_kernel,
        out_shape=(
            jax.ShapeDtypeStruct((tok, model), bf16),
            jax.ShapeDtypeStruct((32, depth, wide), bf16),
        ),
        in_specs=[smem, smem, hbm, hbm, hbm],
        out_specs=(pl.BlockSpec(memory_space=pltpu.VMEM), hbm),
        scratch_shapes=[
            pltpu.VMEM((5, slots, slot_rows, share), bf16),
            pltpu.VMEM((5, slots, slot_rows, share), bf16),
            pltpu.SemaphoreType.DMA((5 * slots,)),
            pltpu.SemaphoreType.DMA((5 * slots,)),
            pltpu.SemaphoreType.DMA((7 * slots,)),
            pltpu.SemaphoreType.DMA((7 * slots,)),
            pltpu.SemaphoreType.DMA((31,)),
            pltpu.SemaphoreType.DMA((31,)),
            pltpu.SemaphoreType.DMA((slots + 2,)),
        ],
        compiler_params=pltpu.CompilerParams(
            collective_id=0, has_side_effects=True, vmem_limit_bytes=24 * 2**20
        ),
        cost_estimate=pl.CostEstimate(flops=0, bytes_accessed=24 * 2**20, transcendentals=0),
    )(bits, live, patches, qkv_w, out_w)


def head_norm(values):
    centred = values - jnp.mean(values, axis=-1, keepdims=True)
    factor = lax.rsqrt(jnp.mean(centred * centred, axis=-1, keepdims=True) + epsilon)
    return centred * factor, factor


def head_norm_back(upstream, normed, factor):
    return factor * (
        upstream
        - jnp.mean(upstream, axis=-1, keepdims=True)
        - normed * jnp.mean(upstream * normed, axis=-1, keepdims=True)
    )


def dot_nn(a, b):
    return jnp.dot(a, b, preferred_element_type=jnp.float32)


def dot_nt(a, b):
    return lax.dot_general(a, b, (((1,), (1,)), ((), ())), preferred_element_type=jnp.float32)


def dot_tn(a, b):
    return lax.dot_general(a, b, (((0,), (0,)), ((), ())), preferred_element_type=jnp.float32)


def exact_dot(a, b, dims):
    return lax.dot_general(
        a, b, (dims, ((), ())),
        precision=lax.Precision.HIGHEST, preferred_element_type=jnp.float32,
    )


def add_into(total, other, rows_at=32):
    @pl.loop(0, total.shape[0] // rows_at)
    def _(i):
        at = pl.ds(pl.multiple_of(i * rows_at, rows_at), rows_at)
        total[at, :] = (
            total[at, :].astype(jnp.float32) + other[at, :].astype(jnp.float32)
        ).astype(total.dtype)


def branch_kernel(
    live_ref, gain, qk_gain, rows_in, weights_in, cotangent,
    attended, grad_rows, grad_qkv_w, grad_out_w,
    rows, weights, upstream, normed, row_mean, row_factor, projected, attention,
    mixed, grad_mixed, grad_qkv, terms, theirs, z_got, y_got, parts, x_got, l_got,
    partial_sums, sums, sums_got,
    core_send, core_recv, z_send_sem, z_recv_sem, y_send, y_recv,
    x_send, x_recv, l_send, l_recv, s_send, s_recv, local_sem,
):
    f32, bf16 = jnp.float32, jnp.bfloat16
    z, yh, c, x, yl = coords()
    me_t = x * 2 + yl
    tok, model = rows.shape
    share = attended.shape[1]
    heads = attention.shape[0]
    slots, slot_rows = attention.shape[1], attention.shape[2]
    head_dim = qk_gain.shape[1]
    qkv_cols, out_cols = grad_qkv_w.shape[1], grad_out_w.shape[1]
    depth = grad_qkv_w.shape[0]
    band = 4 * depth
    z_up, z_down = lax.rem(z + 1, NZ), lax.rem(z + NZ - 1, NZ)
    x_up, x_down = lax.rem(x + 1, NX), lax.rem(x + NX - 1, NX)
    sibling = dev(z, yh, 1 - c, x, yl)
    opposite = dev(z, 1 - yh, c, x, yl)
    beside = dev(z, yh, c, x, 1 - yl)
    up, down = dev(z_up, yh, c, x, yl), dev(z_down, yh, c, x, yl)
    right, left = dev(z, yh, c, x_up, yl), dev(z, yh, c, x_down, yl)
    my_f = z * 4 + yh * 2 + c
    peers = [(my_f, lax.rem(me_t + o, 8)) for o in range(1, 8)]

    loads = [
        pltpu.make_async_copy(rows_in, rows, local_sem.at[0]),
        pltpu.make_async_copy(weights_in, weights, local_sem.at[1]),
        pltpu.make_async_copy(cotangent, upstream, local_sem.at[2]),
    ]
    for copy in loads:
        copy.start()
    greet([sibling, opposite, up, down] + peers)
    sent = []

    def go(copy):
        copy.start()
        sent.append(copy)

    core_sems, z_sems = (core_send, core_recv), (z_send_sem, z_recv_sem)
    y_sems, x_sems, l_sems = (y_send, y_recv), (x_send, x_recv), (l_send, l_recv)
    s_sems = (s_send, s_recv)
    step_rows = 16
    per_slot = slot_rows // step_rows
    qkv_part, out_part = pl.ds(0, qkv_cols), pl.ds(qkv_cols, out_cols)

    def live_rows(i, shape):
        place = lax.broadcasted_iota(jnp.int32, shape, 0) + lax.rem(i, per_slot) * step_rows
        return place < live_ref[lax.div(i, per_slot)]

    loads[0].wait()

    @pl.loop(0, tok // step_rows)
    def _(i):
        at = pl.ds(pl.multiple_of(i * step_rows, step_rows), step_rows)
        values = rows[at, :].astype(f32)
        mean = jnp.mean(values, axis=-1, keepdims=True)
        centred = values - mean
        factor = lax.rsqrt(jnp.mean(centred * centred, axis=-1, keepdims=True) + epsilon)
        normed[at, :] = (centred * factor * gain[...]).astype(bf16)
        row_mean[at, :] = jnp.broadcast_to(mean, (step_rows, 128))
        row_factor[at, :] = jnp.broadcast_to(factor, (step_rows, 128))

    loads[1].wait()
    piece = model // 4

    @pl.loop(0, 4)
    def _(i):
        at = pl.ds(pl.multiple_of(i * piece, piece), piece)
        part = dot_nn(normed[:, at], weights[at, qkv_part])

        @pl.when(i == 0)
        def _():
            projected[...] = part

        @pl.when(i > 0)
        def _():
            projected[...] += part

    query_scale = qk_gain[0:1, :] * head_dim ** (-0.5)
    key_scale = qk_gain[1:2, :]

    def slot_at(s):
        return pl.ds(s * slot_rows, slot_rows)

    def head_at(h, which):
        return pl.ds(pl.multiple_of((h * 3 + which) * head_dim, head_dim), head_dim)

    def mixed_at(h):
        return pl.ds(pl.multiple_of(h * head_dim, head_dim), head_dim)

    def head_rows(h, s):
        query_hat, query_factor = head_norm(projected[slot_at(s), head_at(h, 0)])
        key_hat, key_factor = head_norm(projected[slot_at(s), head_at(h, 1)])
        values = projected[slot_at(s), head_at(h, 2)].astype(bf16)
        return (
            (query_hat, query_factor, (query_hat * query_scale).astype(bf16)),
            (key_hat, key_factor, (key_hat * key_scale).astype(bf16)),
            values,
        )

    @pl.loop(0, heads)
    def _(h):
        i = lax.broadcasted_iota(jnp.int32, (slot_rows, slot_rows), 0)
        j = lax.broadcasted_iota(jnp.int32, (slot_rows, slot_rows), 1)
        for s in range(slots):
            (_, _, query), (_, _, key_rows), values = head_rows(h, s)
            count = live_ref[s]
            allowed = (jnp.maximum(i, j) < count) | (i == j)
            raised = jnp.where(allowed, jnp.exp(dot_nt(query, key_rows)), 0.0)
            weight = raised / jnp.sum(raised, axis=-1, keepdims=True)
            attention[h, s] = weight
            mixed[slot_at(s), mixed_at(h)] = dot_nn(weight.astype(bf16), values).astype(bf16)

    x_limits = {(0, 0): 2, (0, 1): 1, (1, 0): 1, (1, 1): 2}
    x_slot = {}
    for p in range(2):
        for direction in range(2):
            for kind in range(2):
                for d in range(x_limits[direction, kind], 0, -1):
                    x_slot[p, direction, kind, d] = len(x_slot)

    def x_shard(direction, kind, d):
        xx = lax.rem(x + (d if direction == 0 else NX - d), NX)
        return xx * 2 + (yl if kind == 0 else 1 - yl)

    def x_go(p, direction, kind, d):
        slot = x_slot[p, direction, kind, d]
        go(
            remote(
                parts.at[p, x_shard(direction, kind, d)], x_got.at[slot], x_sems, slot,
                right if direction == 0 else left,
            )
        )

    def x_take(p, direction, kind, d):
        slot = x_slot[p, direction, kind, d]
        shard = x_shard(direction, kind, d - 1)
        remote(parts.at[p, shard], x_got.at[slot], x_sems, slot, right).wait_recv()
        add_into(parts.at[p, shard], x_got.at[slot])

    def x_first(p):
        for d in (2, 1):
            for kind in (1, 0):
                for direction in range(2):
                    if d == x_limits[direction, kind]:
                        x_go(p, direction, kind, d)

    def x_second(p):
        x_take(p, 1, 1, 2)
        x_go(p, 1, 1, 1)
        x_take(p, 0, 0, 2)
        x_go(p, 0, 0, 1)

    def x_third(p):
        x_take(p, 0, 1, 1)
        x_take(p, 1, 1, 1)
        go(remote(parts.at[p, x * 2 + 1 - yl], l_got.at[p], l_sems, p, beside))
        x_take(p, 1, 0, 1)
        x_take(p, 0, 0, 1)

    def l_take(p):
        remote(parts.at[p, me_t], l_got.at[p], l_sems, p, beside).wait_recv()

    def shard_rows(shard):
        return pl.ds(pl.multiple_of(shard * share, share), share)

    @pl.loop(0, 8)
    def _(shard):
        parts[0, shard] = dot_nt(mixed[...], weights[shard_rows(shard), out_part]).astype(bf16)

    x_first(0)

    loads[2].wait()

    @pl.loop(0, tok // step_rows)
    def _(i):
        at = pl.ds(pl.multiple_of(i * step_rows, step_rows), step_rows)
        values = upstream[at, :].astype(f32)
        upstream[at, :] = jnp.where(live_rows(i, values.shape), values, 0.0).astype(bf16)

    grad_mixed[...] = dot_nn(upstream[...], weights[:, out_part]).astype(bf16)

    @pl.loop(0, heads)
    def _(h):
        for s in range(slots):
            (query_hat, query_factor, query), (key_hat, key_factor, key_rows), values = head_rows(
                h, s
            )
            weight = attention[h, s]
            rounded = weight.astype(bf16)
            above = grad_mixed[slot_at(s), mixed_at(h)]
            grad_value = dot_tn(rounded, above)
            grad_weight = dot_nt(above, values)
            grad_scores = weight * (
                grad_weight - jnp.sum(weight * grad_weight, axis=-1, keepdims=True)
            )
            grad_scores = grad_scores.astype(bf16)
            grad_query = dot_nn(grad_scores, key_rows)
            grad_key = dot_tn(grad_scores, query)
            grad_qkv[slot_at(s), head_at(h, 0)] = head_norm_back(
                grad_query * query_scale, query_hat, query_factor
            ).astype(bf16)
            grad_qkv[slot_at(s), head_at(h, 1)] = head_norm_back(
                grad_key * key_scale, key_hat, key_factor
            ).astype(bf16)
            grad_qkv[slot_at(s), head_at(h, 2)] = grad_value.astype(bf16)

    def z_at(distance):
        return lax.rem(z + distance + NZ, NZ)

    distances = [4, 3, -3, 2, -2, 1, -1, 0]

    def compute(distance):
        zz = z_at(distance)
        at = pl.ds(pl.multiple_of(zz * band, band), band)
        left_term = dot_tn(normed[:, at], grad_qkv[...]).astype(bf16)
        for q in range(4):
            terms[zz, q // 2, q % 2, :, 0:qkv_cols] = left_term[q * depth : (q + 1) * depth]
        right_term = dot_tn(upstream[:, at], mixed[...]).astype(bf16)
        for q in range(4):
            terms[zz, q // 2, q % 2, :, qkv_cols:] = right_term[q * depth : (q + 1) * depth]
        go(
            remote(
                terms.at[zz, :, 1 - c], theirs.at[zz], core_sems, distances.index(distance), sibling
            )
        )

    def have(distance):
        zz = z_at(distance)
        remote(
            terms.at[zz, :, c], theirs.at[zz], core_sems, distances.index(distance), sibling
        ).wait_recv()
        for y in range(2):
            add_into(terms.at[zz, y, c], theirs.at[zz, y])

    def y_of(kind):
        return yh if kind == 0 else 1 - yh

    limits = {(0, 0): 4, (0, 1): 3, (1, 0): 3, (1, 1): 4}
    z_slot = {}
    for direction in range(2):
        for kind in range(2):
            for d in range(limits[direction, kind], 0, -1):
                z_slot[direction, kind, d] = len(z_slot)

    def z_go(direction, kind, d):
        zz = z_at(d if direction == 0 else -d)
        slot = z_slot[direction, kind, d]
        go(
            remote(
                terms.at[zz, y_of(kind), c], z_got.at[slot], z_sems, slot,
                up if direction == 0 else down,
            )
        )

    def z_take(direction, kind, d):
        zz = z_at(d - 1 if direction == 0 else 1 - d)
        slot = z_slot[direction, kind, d]
        remote(terms.at[zz, y_of(kind), c], z_got.at[slot], z_sems, slot, up).wait_recv()
        add_into(terms.at[zz, y_of(kind), c], z_got.at[slot])

    def z_pass(direction, kind, d):
        z_take(direction, kind, d)
        z_go(direction, kind, d - 1)

    compute(4)
    compute(3)
    have(4)
    z_go(1, 1, 4)
    z_go(0, 0, 4)
    compute(-3)
    have(3)
    z_go(0, 1, 3)
    compute(2)
    have(-3)
    z_go(1, 0, 3)
    x_second(0)

    partial_sums[...] = jnp.zeros(partial_sums.shape, f32)

    @pl.loop(0, 8)
    def _(shard):
        at = shard_rows(shard)
        part = dot_nt(grad_qkv[...], weights[at, qkv_part]).astype(bf16)
        parts[1, shard] = part
        scaled = part.astype(f32) * gain[:, at]
        for q in range(share // 128):
            lanes = slice(q * 128, (q + 1) * 128)
            own = pl.ds(pl.multiple_of(shard * share + q * 128, 128), 128)
            centred = (rows[:, own].astype(f32) - row_mean[...]) * row_factor[...]
            partial_sums[0] += scaled[:, lanes]
            partial_sums[1] += scaled[:, lanes] * centred

    x_first(1)
    ones = jnp.ones((8, 128), f32)
    upper = lax.broadcasted_iota(jnp.int32, (8, tok), 0) < 4
    sums[...] = jnp.where(
        upper,
        exact_dot(ones, partial_sums[0], ((1,), (1,))),
        exact_dot(ones, partial_sums[1], ((1,), (1,))),
    )
    for o, peer in enumerate(peers):
        go(remote(sums, sums_got.at[o], s_sems, o, peer))

    z_pass(1, 1, 4)
    z_pass(0, 0, 4)
    compute(-2)
    have(2)
    z_pass(0, 1, 3)
    compute(1)
    have(-2)
    z_pass(1, 0, 3)
    x_third(0)
    compute(-1)
    compute(0)
    have(1)
    z_pass(1, 1, 3)
    z_pass(0, 0, 3)
    have(-1)
    have(0)
    x_second(1)
    z_pass(0, 1, 2)
    z_pass(1, 0, 2)
    l_take(0)

    @pl.loop(0, tok // step_rows)
    def _(i):
        at = pl.ds(pl.multiple_of(i * step_rows, step_rows), step_rows)
        total = parts[0, me_t, at, :].astype(f32) + l_got[0, at, :].astype(f32)
        attended[at, :] = jnp.where(live_rows(i, total.shape), total, 0.0).astype(bf16)

    z_pass(1, 1, 2)
    z_pass(0, 0, 2)
    x_third(1)
    total_sums = sums[...]
    for o, peer in enumerate(peers):
        remote(sums, sums_got.at[o], s_sems, o, peer).wait_recv()
        total_sums += sums_got[o]
    pick = lax.broadcasted_iota(jnp.int32, (8, 128), 0)
    partial_sums[0] = exact_dot(
        total_sums, jnp.where(pick == 0, 1.0 / model, 0.0).astype(f32), ((0,), (0,))
    )
    partial_sums[1] = exact_dot(
        total_sums, jnp.where(pick == 4, 1.0 / model, 0.0).astype(f32), ((0,), (0,))
    )
    z_take(0, 1, 1)
    z_take(1, 1, 1)
    go(remote(terms.at[z, 1 - yh, c], y_got, y_sems, 0, opposite))
    l_take(1)

    @pl.loop(0, tok // step_rows)
    def _(i):
        at = pl.ds(pl.multiple_of(i * step_rows, step_rows), step_rows)
        for q in range(share // 128):
            lanes = slice(q * 128, (q + 1) * 128)
            own = pl.ds(pl.multiple_of(me_t * share + q * 128, 128), 128)
            total = parts[1, me_t, at, lanes].astype(f32) + l_got[1, at, lanes].astype(f32)
            centred = (rows[at, own].astype(f32) - row_mean[at, :]) * row_factor[at, :]
            grad_rows[at, lanes] = (
                row_factor[at, :]
                * (total * gain[:, own] - partial_sums[0, at, :] - centred * partial_sums[1, at, :])
            ).astype(bf16)

    z_take(1, 0, 1)
    z_take(0, 0, 1)
    remote(terms.at[z, yh, c], y_got, y_sems, 0, opposite).wait_recv()

    @pl.loop(0, depth // step_rows)
    def _(i):
        at = pl.ds(pl.multiple_of(i * step_rows, step_rows), step_rows)
        total = terms[z, yh, c, at, :].astype(f32) + y_got[at, :].astype(f32)
        grad_qkv_w[at, :] = total[:, :qkv_cols]
        grad_out_w[at, :] = total[:, qkv_cols:]

    for copy in sent:
        copy.wait_send()


def branch(live, gain, qk_gain, rows, weights, cotangent, qkv_cols):
    bf16, f32 = jnp.bfloat16, jnp.float32
    tok, model = rows.shape
    wide = weights.shape[1]
    out_cols = wide - qkv_cols
    depth = model // 32
    share = model // 8
    head_dim = qk_gain.shape[1]
    heads = out_cols // head_dim
    slots = live.shape[0]
    slot_rows = tok // slots
    hbm = pl.BlockSpec(memory_space=pl.ANY)
    vmem = pl.BlockSpec(memory_space=pltpu.VMEM)
    smem = pl.BlockSpec(memory_space=pltpu.SMEM)
    dma = pltpu.SemaphoreType.DMA
    sems = []
    for n in (8, 14, 1, 12, 2, 7):
        sems += [dma((n,)), dma((n,))]
    return pl.pallas_call(
        branch_kernel,
        out_shape=(
            jax.ShapeDtypeStruct((tok, share), bf16),
            jax.ShapeDtypeStruct((tok, share), bf16),
            jax.ShapeDtypeStruct((depth, qkv_cols), f32),
            jax.ShapeDtypeStruct((depth, out_cols), f32),
        ),
        in_specs=[smem, vmem, vmem, hbm, hbm, hbm],
        out_specs=(vmem,) * 4,
        scratch_shapes=[
            pltpu.VMEM((tok, model), bf16),
            pltpu.VMEM((model, wide), bf16),
            pltpu.VMEM((tok, model), bf16),
            pltpu.VMEM((tok, model), bf16),
            pltpu.VMEM((tok, 128), f32),
            pltpu.VMEM((tok, 128), f32),
            pltpu.VMEM((tok, qkv_cols), f32),
            pltpu.VMEM((heads, slots, slot_rows, slot_rows), f32),
            pltpu.VMEM((tok, out_cols), bf16),
            pltpu.VMEM((tok, out_cols), bf16),
            pltpu.VMEM((tok, qkv_cols), bf16),
            pltpu.VMEM((NZ, 2, 2, depth, wide), bf16),
            pltpu.VMEM((NZ, 2, depth, wide), bf16),
            pltpu.VMEM((14, depth, wide), bf16),
            pltpu.VMEM((depth, wide), bf16),
            pltpu.VMEM((2, 8, tok, share), bf16),
            pltpu.VMEM((12, tok, share), bf16),
            pltpu.VMEM((2, tok, share), bf16),
            pltpu.VMEM((2, tok, 128), f32),
            pltpu.VMEM((8, tok), f32),
            pltpu.VMEM((7, 8, tok), f32),
        ]
        + sems
        + [dma((3,))],
        compiler_params=pltpu.CompilerParams(
            collective_id=1, has_side_effects=True, vmem_limit_bytes=60 * 2**20
        ),
        cost_estimate=pl.CostEstimate(
            flops=13 * 10**9, bytes_accessed=16 * 2**20, transcendentals=150528
        ),
    )(live, gain, qk_gain, rows, weights, cotangent)


def per_device(patches, cotangent, counts, masks, norm_gain, qk_gain, qkv_weight, out_weight):
    replicas = lax.axis_size("fsdp")
    my_replica = lax.axis_index("fsdp")
    qkv_cols = qkv_weight.shape[1]
    bit = [jnp.bitwise_and(jnp.right_shift(masks, place), 1) for place in range(5)]
    bits = jnp.stack(
        [bit[1], bit[4], bit[3] ^ bit[4], bit[2] ^ bit[3], bit[0]], axis=1
    ).astype(jnp.int32)
    replica_ids = jnp.arange(replicas, dtype=jnp.int32)
    sources = jnp.bitwise_xor(my_replica, masks)
    run_counts = jnp.sum(jnp.where(replica_ids[:, None] == sources[None, :], counts, 0), axis=0)
    run_counts = run_counts.astype(jnp.int32)
    block_rows, weights = gather(bits, run_counts, patches, qkv_weight, out_weight)
    weights = weights.reshape(norm_gain.shape[0], qkv_cols + out_weight.shape[1])
    return branch(
        run_counts, norm_gain[None, :], qk_gain, block_rows, weights, cotangent, qkv_cols
    )


def solution(mesh):
    in_specs = (
        P("fsdp", None),
        P("fsdp", None),
        P(),
        P(),
        P(),
        P(),
        P("fsdp", "tp"),
        P("fsdp", "tp"),
    )
    out_specs = (P("fsdp", "tp"), P("fsdp", "tp"), P("fsdp", "tp"), P("fsdp", "tp"))
    return jax.shard_map(
        per_device, mesh=mesh, in_specs=in_specs, out_specs=out_specs, check_vma=False
    )
```

time: 289 us -> 213 us (0.74)
  matrix products: 47.7 us -> 0 us
  Pallas kernels: 176 us -> 193 us
  blocking collectives: 16.8 us -> 0 us
  other arithmetic: 15.4 us -> 1.53 us
  local copies, waits for them, and re-layouts: 29.4 us -> 16.1 us
    dot_general x11 -> x0, matrix products: 44.5 us -> none  [the longest x1 11.6 us: per_device(): lax.dot_general(grad_qkv, qkv_full, (((1,), (1,)), ((), ())), preferred_e...]
    psum x1 -> x0, blocking collectives: 16.8 us -> none  [per_device(): sums = lax.psum(sums, 'tp') / model_width]
    pallas_call x1, Pallas kernels: 72.1 us -> 88.8 us  [branch(): pl.pallas_call(branch_kernel, out_shape=(jax.ShapeDtypeStruct((tok, share...]
    reshape x3 -> x0, local copies, waits for them, and re-layouts: 6.31 us -> none  [the longest x1 4.05 us: per_device(): jnp.dot(normed, qkv_full, preferred_element_type=jnp.float32)]
    reduce_sum x5 -> x0, other arithmetic: 5.3 us -> none  [the longest x2 3.45 us: norm_rows(): row_mean = jnp.mean(values, axis=-1, keepdims=True)]
    convert_element_type x2 -> x0, local copies, waits for them, and re-layouts: 4.56 us -> none  [the longest x1 3.34 us: per_device(): grad_qkv = jnp.stack([query_grad, key_grad, grad_value], axis=3).astype(j...]
    unnamed x39 -> x16, local copies, waits for them, and re-layouts: 11 us -> 15.6 us
    convert_element_type x3 -> x0, other arithmetic: 4.46 us -> none  [the longest x1 2.07 us: per_device(): grad_rows = grad_rows.astype(jnp.bfloat16)]
where the time goes in v2:
time: 213 us; the launch traced here: 211 us
  Pallas kernels  193 us (91%)
  local copies, waits for them, and re-layouts  16.1 us (8%)
    pallas_call x1, Pallas kernels, gather(): pl.pallas_call(gather_kernel, out_shape=(jax.ShapeDtypeStruct((tok, model...  104 us
    pallas_call x1, Pallas kernels, branch(): pl.pallas_call(branch_kernel, out_shape=(jax.ShapeDtypeStruct((tok, share...  88.8 us
    unnamed x16, local copies, waits for them, and re-layouts  15.6 us

profile of v2, /device:TPU:2, one launch (start us, length us, event | category | flops | bytes accessed | tf_op | source)
XLA Modules:
  0.0 210.9 jit_solution(12415046801386375071)
XLA Ops:
  0.6 0.7 and_bitcast_fusion
  1.3 0.9 select_reduce_fusion.live_ref
  2.2 0.0 copy-start.3
  2.2 0.1 copy.16
  2.3 0.1 copy.14
  2.4 0.1 copy.13
  2.4 0.1 copy.12
  2.5 0.1 copy.15
  2.6 0.1 stack.23.bits_ref
  2.7 0.0 copy-start
  2.7 1.8 copy-done
  4.5 0.0 copy-start.1
  4.5 0.9 copy-done.1
  5.4 0.0 copy-start.2
  5.4 0.9 copy-done.2
  6.3 103.8 %shard_map.111 = (bf16[448,3072]{1,0:T(8,128)(2,1)S(1)}, bf16[32,96,1536]{2,1,0:T(8,128)(2,1)S(1)}) custom-call(s32[4,5]{1,0:T(4,128)S(1)} %stack.23.bits_ref, s32[4]{0:T(128)S(1)} %select_reduce_fusion.live_ref, bf16[448,3072]{1,0:T(8,128)(2,1)S(1)} %copy-done, bf16[96,1152]{1,0:T(8,128)(2,1)S(1)} %copy-done.1, bf16[96,384]{1,0:T(8,128)(2,1)S(1)} %copy-done.2), custom_call_target="tpu_custom_call" | custom-call | bytes 25165824 | tf_op jit(solution)/shard_map/pallas_call | solution.py:232
  110.1 0.0 copy-start.4
  110.2 3.6 %copy-done.4 = bf16[32,96,1536]{2,1,0:T(8,128)(2,1)} copy-done((bf16[32,96,1536]{2,1,0:T(8,128)(2,1)}, bf16[32,96,1536]{2,1,0:T(8,128)(2,1)S(1)}, u32[]{:S(2)}) %copy-start.4) | copy-done | bytes 9437208
  113.8 0.0 copy-start.5
  113.8 1.5 copy-done.5
  115.3 0.0 copy-done.3
  115.3 88.8 %shard_map.112 = (bf16[448,384]{1,0:T(8,128)(2,1)}, bf16[448,384]{1,0:T(8,128)(2,1)}, f32[96,1152]{1,0:T(8,128)}, f32[96,384]{1,0:T(8,128)}) custom-call(s32[4]{0:T(128)} %copy-done.3, f32[1,3072]{1,0:T(1,128)} %bitcast.13, f32[2,128]{1,0:T(2,128)} %qk_gain.1, bf16[448,3072]{1,0:T(8,128)(2,1)} %copy-done.5, bf16[3072,1536]{1,0:T(8,128)(2,1)} %bitcast.12, ...), custom_call_target="tpu_custom_call" | custom-call | flops 12999999488 | bytes 16777216 | tf_op jit(solution)/shard_map/pallas_call | solution.py:702
  204.1 1.7 copy.21
  205.8 1.7 copy.22
  207.6 1.8 copy.23
  209.4 1.6 copy.24
Async XLA Ops:
  2.2 113.1 %copy-start.3 = (s32[4]{0:T(128)}, s32[4]{0:T(128)S(1)}, u32[]{:S(2)}) copy-start(s32[4]{0:T(128)S(1)} %select_reduce_fusion.live_ref) | copy-start | bytes 52
  2.7 1.8 copy-start
  4.5 0.9 copy-start.1
  5.4 0.9 copy-start.2
  110.1 3.6 %copy-start.4 = (bf16[32,96,1536]{2,1,0:T(8,128)(2,1)}, bf16[32,96,1536]{2,1,0:T(8,128)(2,1)S(1)}, u32[]{:S(2)}) copy-start(bf16[32,96,1536]{2,1,0:T(8,128)(2,1)S(1)} %get-tuple-element.7) | copy-start | bytes 28311556
  113.8 1.5 copy-start.5

commit v3 on v2

v3 whole, which is shorter than its diff:
```python
import functools
import jax
import jax.numpy as jnp
from jax import lax
from jax.experimental import pallas as pl
from jax.experimental.pallas import tpu as pltpu
from jax.sharding import PartitionSpec as P

MESH = pl.DeviceIdType.MESH
epsilon = 1e-06
NZ, NX = 8, 4
W_ROWS, G_ROWS = 32, 48


def coords():
    f = lax.axis_index("fsdp")
    t = lax.axis_index("tp")
    z, yh, c = lax.div(f, 4), lax.rem(lax.div(f, 2), 2), lax.rem(f, 2)
    x, yl = lax.div(t, 2), lax.rem(t, 2)
    return z, yh, c, x, yl


def dev(z, yh, c, x, yl):
    return (z * 4 + yh * 2 + c, x * 2 + yl)


def remote(src, dst, sems, slot, target):
    send, recv = sems
    return pltpu.make_async_remote_copy(
        src_ref=src,
        dst_ref=dst,
        send_sem=send.at[slot],
        recv_sem=recv.at[slot],
        device_id=target,
        device_id_type=MESH,
    )


def greet(partners):
    barrier = pltpu.get_barrier_semaphore()
    for partner in partners:
        pl.semaphore_signal(barrier, inc=1, device_id=partner, device_id_type=MESH)
    pl.semaphore_wait(barrier, len(partners))


def head_norm(values):
    centred = values - jnp.mean(values, axis=-1, keepdims=True)
    factor = lax.rsqrt(jnp.mean(centred * centred, axis=-1, keepdims=True) + epsilon)
    return centred * factor, factor


def head_norm_back(upstream, normed, factor):
    return factor * (
        upstream
        - jnp.mean(upstream, axis=-1, keepdims=True)
        - normed * jnp.mean(upstream * normed, axis=-1, keepdims=True)
    )


def dot_nn(a, b):
    return jnp.dot(a, b, preferred_element_type=jnp.float32)


def dot_nt(a, b):
    return lax.dot_general(a, b, (((1,), (1,)), ((), ())), preferred_element_type=jnp.float32)


def dot_tn(a, b):
    return lax.dot_general(a, b, (((0,), (0,)), ((), ())), preferred_element_type=jnp.float32)


def exact_dot(a, b, dims):
    return lax.dot_general(
        a, b, (dims, ((), ())),
        precision=lax.Precision.HIGHEST, preferred_element_type=jnp.float32,
    )


def add_into(total, other, rows_at=32):
    @pl.loop(0, total.shape[0] // rows_at)
    def _(i):
        at = pl.ds(pl.multiple_of(i * rows_at, rows_at), rows_at)
        total[at, :] = (
            total[at, :].astype(jnp.float32) + other[at, :].astype(jnp.float32)
        ).astype(total.dtype)


def branch_kernel(
    bits_ref, live_ref, gain, qk_gain, patches, cotangent, qkv_w, out_w,
    attended, grad_rows, grad_qkv_w, grad_out_w,
    hold, got, rows, weights, upstream, normed, row_mean, row_factor, projected, attention,
    mixed, grad_mixed, grad_qkv, terms, theirs, y_part, z_got, y_got, parts, x_got, l_got,
    partial_sums, sums, sums_got,
    a_send, a_recv, b_send, b_recv, c_send, c_recv,
    core_send, core_recv, z_send_sem, z_recv_sem, y_send, y_recv,
    x_send, x_recv, l_send, l_recv, s_send, s_recv, local_sem,
):
    f32, bf16 = jnp.float32, jnp.bfloat16
    z, yh, c, x, yl = coords()
    me_t = x * 2 + yl
    tok, model = rows.shape
    share = attended.shape[1]
    heads = attention.shape[0]
    slots, slot_rows = attention.shape[1], attention.shape[2]
    head_dim = qk_gain.shape[1]
    qkv_cols, out_cols = grad_qkv_w.shape[1], grad_out_w.shape[1]
    depth = grad_qkv_w.shape[0]
    band = 4 * depth
    z_up, z_down = lax.rem(z + 1, NZ), lax.rem(z + NZ - 1, NZ)
    x_up, x_down = lax.rem(x + 1, NX), lax.rem(x + NX - 1, NX)
    sibling = dev(z, yh, 1 - c, x, yl)
    opposite = dev(z, 1 - yh, c, x, yl)
    beside = dev(z, yh, c, x, 1 - yl)
    up, down = dev(z_up, yh, c, x, yl), dev(z_down, yh, c, x, yl)
    right, left = dev(z, yh, c, x_up, yl), dev(z, yh, c, x_down, yl)
    across = dev(z, 1 - yh, c, x, 1 - yl)
    z7 = dev(7 - z, yh, c, x, yl)
    z3 = dev(z + 3 - 2 * lax.rem(z, 4), yh, c, x, yl)
    z1 = dev(z + 1 - 2 * lax.rem(z, 2), yh, c, x, yl)
    my_f = z * 4 + yh * 2 + c
    peers = [(my_f, lax.rem(me_t + o, 8)) for o in range(1, 8)]
    f32, bf16 = jnp.float32, jnp.bfloat16

    def slot_at(s):
        return pl.ds(s * slot_rows, slot_rows)

    def columns(index):
        return pl.ds(pl.multiple_of(index * share, 128), share)

    def weight_at(index, first, count):
        return weights.at[pl.ds(pl.multiple_of(index * depth + first, 16), count), :]

    own = [
        pltpu.make_async_copy(patches.at[slot_at(k), columns(me_t)], hold.at[0, k], local_sem.at[k])
        for k in range(slots)
    ]
    mine = pl.ds(pl.multiple_of(my_f * depth, 16), depth)
    own_w = [
        pltpu.make_async_copy(qkv_w, weights.at[mine, pl.ds(0, qkv_cols)], local_sem.at[slots]),
        pltpu.make_async_copy(
            out_w, weights.at[mine, pl.ds(qkv_cols, out_cols)], local_sem.at[slots + 1]
        ),
    ]
    load = pltpu.make_async_copy(cotangent, upstream, local_sem.at[slots + 2])
    for copy in own_w + own + [load]:
        copy.start()
    greet([across, z7, z3, z1, sibling, opposite, up, down] + peers)
    sent = []

    def go(copy):
        copy.start()
        sent.append(copy)

    a_sems, b_sems, c_sems = (a_send, a_recv), (b_send, b_recv), (c_send, c_recv)
    core_sems, z_sems = (core_send, core_recv), (z_send_sem, z_recv_sem)
    y_sems, x_sems, l_sems = (y_send, y_recv), (x_send, x_recv), (l_send, l_recv)
    s_sems = (s_send, s_recv)
    step_rows = 16
    per_slot = slot_rows // step_rows
    qkv_part, out_part = pl.ds(0, qkv_cols), pl.ds(qkv_cols, out_cols)
    limits = {(0, 0): 4, (0, 1): 3, (1, 0): 3, (1, 1): 4}

    def z_at(distance):
        return lax.rem(z + distance + NZ, NZ)

    def y_of(kind):
        return yh if kind == 0 else 1 - yh

    w_slot = {}

    def w_index(key):
        if key not in w_slot:
            w_slot[key] = len(w_slot)
        return w_slot[key]

    def w_copy(route, piece, target, core=0):
        distance, kind, first, count = piece
        owner = z_at(distance) * 4 + y_of(kind) * 2 + (1 - c if core else c)
        view = weight_at(owner, first, count)
        return remote(view, view, c_sems, w_index((route, piece)), target)

    def w_core(piece):
        go(w_copy("core", piece, sibling))

    def w_core_take(piece):
        w_copy("core", piece, sibling, 1).wait_recv()

    def w_rows(kind):
        return (0, depth) if kind == 0 else (0, W_ROWS)

    rest = (W_ROWS, depth - W_ROWS)

    def w_route(direction):
        return "up" if direction == 0 else "down"

    def w_send(direction, kind, travelled):
        signed = -travelled if direction == 0 else travelled
        first, count = w_rows(kind)
        owner = z_at(signed) * 4 + y_of(kind) * 2 + c
        view = weight_at(owner, first, count)
        there = -travelled - 1 if direction == 0 else travelled + 1
        slot = w_index((w_route(direction), (there, kind, first, count)))
        go(remote(view, view, c_sems, slot, up if direction == 0 else down))

    def w_take(direction, kind, d):
        signed = -d if direction == 0 else d
        piece = (signed, kind) + w_rows(kind)
        w_copy(w_route(direction), piece, up).wait_recv()
        if d < limits[direction, kind]:
            w_send(direction, kind, d)
        if kind == 0:
            owner = z_at(signed) * 4 + yh * 2 + c
            view = weight_at(owner, *rest)
            go(remote(view, view, c_sems, w_index(("y", (signed, 1) + rest)), opposite))
        w_core(piece)

    def w_round(d):
        for kind in range(2):
            for direction in range(2):
                if d <= limits[direction, kind]:
                    w_take(direction, kind, d)

    def w_across(signed):
        piece = (signed, 1) + rest
        w_copy("y", piece, opposite).wait_recv()
        w_core(piece)

    for k in range(slots):
        go(remote(patches.at[slot_at(k), columns(x * 2 + 1 - yl)], got.at[0, k], a_sems, k, across))
    for copy in own_w:
        copy.wait()
    whole = (0, depth)
    view = weight_at(my_f, *whole)
    go(remote(view, view, c_sems, w_index(("y", (0, 1) + whole)), opposite))
    w_core((0, 0) + whole)
    w_send(0, 0, 0)
    w_send(1, 0, 0)
    for copy in own:
        copy.wait()

    partner = {3: z3, 7: z7, 1: z1, 0: sibling}
    bit_column = {7: 1, 3: 2, 1: 3, 0: 4}
    order = [[7, 3, 1, 0], [3, 7, 1, 0], [7, 3, 1, 0], [3, 7, 1, 0]]

    def merge(k, step):
        remote(got.at[step, k], got.at[step, k], a_sems, step * slots + k, sibling).wait_recv()
        taken = bits_ref[k, 0 if step == 0 else bit_column[order[k][step - 1]]] > 0
        return lax.select_n(taken, hold[step, k], got[step, k])

    def row_step(step):
        for k in range(slots):
            hold[step + 1, k] = merge(k, step)
            go(
                remote(
                    hold.at[step + 1, k], got.at[step + 1, k], a_sems,
                    (step + 1) * slots + k, partner[order[k][step]],
                )
            )

    def row_copy(k, xx, y_low, which, target):
        view = rows.at[slot_at(k), columns(xx * 2 + y_low)]
        return remote(view, view, b_sems, k * 7 + which, target)

    def rows_first(k):
        merged = merge(k, 4).astype(f32)
        place = lax.broadcasted_iota(jnp.int32, (slot_rows, share), 0)
        live = place < live_ref[k]
        rows[slot_at(k), columns(me_t)] = jnp.where(live, merged, 0.0).astype(bf16)
        go(row_copy(k, x, yl, 0, beside))
        go(row_copy(k, x, yl, 1, right))
        go(row_copy(k, x, yl, 4, left))

    def rows_second(k):
        row_copy(k, x, 1 - yl, 0, beside).wait_recv()
        go(row_copy(k, x, 1 - yl, 3, right))
        go(row_copy(k, x, 1 - yl, 5, left))

    def rows_third(k):
        row_copy(k, x_down, yl, 1, right).wait_recv()
        go(row_copy(k, x_down, yl, 2, right))
        row_copy(k, x_up, 1 - yl, 5, left).wait_recv()
        go(row_copy(k, x_up, 1 - yl, 6, left))

    def rows_last(k):
        row_copy(k, lax.rem(x + 2, NX), yl, 2, right).wait_recv()
        row_copy(k, x_down, 1 - yl, 3, right).wait_recv()
        row_copy(k, x_up, yl, 4, left).wait_recv()
        row_copy(k, lax.rem(x + 2, NX), 1 - yl, 6, left).wait_recv()

    def norm_slot(k):
        @pl.loop(0, per_slot)
        def _(i):
            at = pl.ds(pl.multiple_of(k * slot_rows + i * step_rows, step_rows), step_rows)
            values = rows[at, :].astype(f32)
            mean = jnp.mean(values, axis=-1, keepdims=True)
            centred = values - mean
            factor = lax.rsqrt(jnp.mean(centred * centred, axis=-1, keepdims=True) + epsilon)
            normed[at, :] = (centred * factor * gain[...]).astype(bf16)
            row_mean[at, :] = jnp.broadcast_to(mean, (step_rows, 128))
            row_factor[at, :] = jnp.broadcast_to(factor, (step_rows, 128))

    def project(distance):
        if distance == 0:
            for kind in range(2):
                w_core_take((0, kind) + whole)
        else:
            for kind, part in ((0, whole), (1, (0, W_ROWS)), (1, rest)):
                signed = distance
                if abs(distance) == 4:
                    signed = 4 if (kind, part) == (1, (0, W_ROWS)) else -4
                w_core_take((signed, kind) + part)
        at = pl.ds(pl.multiple_of(z_at(distance) * band, band), band)
        part = dot_nn(normed[:, at], weights[at, qkv_part])
        if distance == 0:
            projected[...] = part
        else:
            projected[...] += part

    def live_rows(i, shape):
        place = lax.broadcasted_iota(jnp.int32, shape, 0) + lax.rem(i, per_slot) * step_rows
        return place < live_ref[lax.div(i, per_slot)]

    row_step(0)
    w_copy("y", (0, 1) + whole, opposite).wait_recv()
    w_send(0, 1, 0)
    w_send(1, 1, 0)
    w_core((0, 1) + whole)
    row_step(1)
    w_round(1)
    row_step(2)
    w_across(-1)
    w_across(1)
    row_step(3)
    w_round(2)
    for k in range(slots):
        rows_first(k)
    for k in range(slots):
        rows_second(k)
    w_across(-2)
    w_across(2)
    for k in range(slots):
        rows_third(k)
    w_round(3)
    load.wait()

    @pl.loop(0, tok // step_rows)
    def _(i):
        at = pl.ds(pl.multiple_of(i * step_rows, step_rows), step_rows)
        values = upstream[at, :].astype(f32)
        upstream[at, :] = jnp.where(live_rows(i, values.shape), values, 0.0).astype(bf16)

    for k in range(slots):
        rows_last(k)
        norm_slot(k)
    project(0)
    project(-1)
    project(1)
    w_across(-3)
    w_across(3)
    project(-2)
    project(2)
    w_round(4)
    project(-3)
    project(3)
    w_across(-4)
    project(4)

    query_scale = qk_gain[0:1, :] * head_dim ** (-0.5)
    key_scale = qk_gain[1:2, :]

    def head_at(h, which):
        return pl.ds(pl.multiple_of((h * 3 + which) * head_dim, head_dim), head_dim)

    def mixed_at(h):
        return pl.ds(pl.multiple_of(h * head_dim, head_dim), head_dim)

    def head_rows(h, s):
        query_hat, query_factor = head_norm(projected[slot_at(s), head_at(h, 0)])
        key_hat, key_factor = head_norm(projected[slot_at(s), head_at(h, 1)])
        values = projected[slot_at(s), head_at(h, 2)].astype(bf16)
        return (
            (query_hat, query_factor, (query_hat * query_scale).astype(bf16)),
            (key_hat, key_factor, (key_hat * key_scale).astype(bf16)),
            values,
        )

    @pl.loop(0, heads)
    def _(h):
        i = lax.broadcasted_iota(jnp.int32, (slot_rows, slot_rows), 0)
        j = lax.broadcasted_iota(jnp.int32, (slot_rows, slot_rows), 1)
        for s in range(slots):
            (_, _, query), (_, _, key_rows), values = head_rows(h, s)
            count = live_ref[s]
            allowed = (jnp.maximum(i, j) < count) | (i == j)
            raised = jnp.where(allowed, jnp.exp(dot_nt(query, key_rows)), 0.0)
            weight = raised / jnp.sum(raised, axis=-1, keepdims=True)
            attention[h, s] = weight
            mixed[slot_at(s), mixed_at(h)] = dot_nn(weight.astype(bf16), values).astype(bf16)

    x_limits = {(0, 0): 2, (0, 1): 1, (1, 0): 1, (1, 1): 2}
    x_slot = {}
    for p in range(2):
        for direction in range(2):
            for kind in range(2):
                for d in range(x_limits[direction, kind], 0, -1):
                    x_slot[p, direction, kind, d] = len(x_slot)

    def x_shard(direction, kind, d):
        xx = lax.rem(x + (d if direction == 0 else NX - d), NX)
        return xx * 2 + (yl if kind == 0 else 1 - yl)

    def x_go(p, direction, kind, d):
        slot = x_slot[p, direction, kind, d]
        go(
            remote(
                parts.at[p, x_shard(direction, kind, d)], x_got.at[slot], x_sems, slot,
                right if direction == 0 else left,
            )
        )

    def x_take(p, direction, kind, d):
        slot = x_slot[p, direction, kind, d]
        shard = x_shard(direction, kind, d - 1)
        remote(parts.at[p, shard], x_got.at[slot], x_sems, slot, right).wait_recv()
        add_into(parts.at[p, shard], x_got.at[slot])

    def x_first(p):
        for d in (2, 1):
            for kind in (1, 0):
                for direction in range(2):
                    if d == x_limits[direction, kind]:
                        x_go(p, direction, kind, d)

    def x_second(p):
        x_take(p, 1, 1, 2)
        x_go(p, 1, 1, 1)
        x_take(p, 0, 0, 2)
        x_go(p, 0, 0, 1)

    def x_third(p):
        x_take(p, 0, 1, 1)
        x_take(p, 1, 1, 1)
        go(remote(parts.at[p, x * 2 + 1 - yl], l_got.at[p], l_sems, p, beside))
        x_take(p, 1, 0, 1)
        x_take(p, 0, 0, 1)

    def l_take(p):
        remote(parts.at[p, me_t], l_got.at[p], l_sems, p, beside).wait_recv()

    def shard_rows(shard):
        return pl.ds(pl.multiple_of(shard * share, share), share)

    @pl.loop(0, 8)
    def _(shard):
        parts[0, shard] = dot_nt(mixed[...], weights[shard_rows(shard), out_part]).astype(bf16)

    x_first(0)

    grad_mixed[...] = dot_nn(upstream[...], weights[:, out_part]).astype(bf16)

    @pl.loop(0, heads)
    def _(h):
        for s in range(slots):
            (query_hat, query_factor, query), (key_hat, key_factor, key_rows), values = head_rows(
                h, s
            )
            weight = attention[h, s]
            rounded = weight.astype(bf16)
            above = grad_mixed[slot_at(s), mixed_at(h)]
            grad_value = dot_tn(rounded, above)
            grad_weight = dot_nt(above, values)
            grad_scores = weight * (
                grad_weight - jnp.sum(weight * grad_weight, axis=-1, keepdims=True)
            )
            grad_scores = grad_scores.astype(bf16)
            grad_query = dot_nn(grad_scores, key_rows)
            grad_key = dot_tn(grad_scores, query)
            grad_qkv[slot_at(s), head_at(h, 0)] = head_norm_back(
                grad_query * query_scale, query_hat, query_factor
            ).astype(bf16)
            grad_qkv[slot_at(s), head_at(h, 1)] = head_norm_back(
                grad_key * key_scale, key_hat, key_factor
            ).astype(bf16)
            grad_qkv[slot_at(s), head_at(h, 2)] = grad_value.astype(bf16)

    distances = [4, 3, -3, 2, -2, 1, -1, 0]
    kept = pl.ds(0, G_ROWS)
    crossing = pl.ds(G_ROWS, depth - G_ROWS)

    def compute(distance):
        zz = z_at(distance)
        at = pl.ds(pl.multiple_of(zz * band, band), band)
        left_term = dot_tn(normed[:, at], grad_qkv[...]).astype(bf16)
        for q in range(4):
            terms[zz, q // 2, q % 2, :, 0:qkv_cols] = left_term[q * depth : (q + 1) * depth]
        right_term = dot_tn(upstream[:, at], mixed[...]).astype(bf16)
        for q in range(4):
            terms[zz, q // 2, q % 2, :, qkv_cols:] = right_term[q * depth : (q + 1) * depth]
        go(
            remote(
                terms.at[zz, :, 1 - c], theirs.at[zz], core_sems, distances.index(distance), sibling
            )
        )

    def have(distance):
        i = distances.index(distance)
        zz = z_at(distance)
        remote(terms.at[zz, :, c], theirs.at[zz], core_sems, i, sibling).wait_recv()
        add_into(terms.at[zz, 1 - yh, c], theirs.at[zz, 1 - yh])
        target = y_got.at[crossing] if distance == 0 else y_part.at[i]
        go(remote(terms.at[zz, 1 - yh, c, crossing], target, y_sems, i, opposite))
        add_into(terms.at[zz, yh, c], theirs.at[zz, yh])

    def y_take(distance):
        i = distances.index(distance)
        zz = z_at(distance)
        remote(terms.at[zz, yh, c, crossing], y_part.at[i], y_sems, i, opposite).wait_recv()
        add_into(terms.at[zz, yh, c, crossing], y_part.at[i], 16)

    z_slot = {}
    for direction in range(2):
        for kind in range(2):
            for d in range(limits[direction, kind], 0, -1):
                z_slot[direction, kind, d] = len(z_slot)

    def z_views(kind, zz, slot):
        if kind == 0:
            return terms.at[zz, yh, c], z_got.at[slot]
        return terms.at[zz, 1 - yh, c, kept], z_got.at[slot, kept]

    def z_go(direction, kind, d):
        zz = z_at(d if direction == 0 else -d)
        slot = z_slot[direction, kind, d]
        here, there = z_views(kind, zz, slot)
        go(remote(here, there, z_sems, slot, up if direction == 0 else down))

    def z_take(direction, kind, d):
        zz = z_at(d - 1 if direction == 0 else 1 - d)
        slot = z_slot[direction, kind, d]
        here, arrived = z_views(kind, zz, slot)
        remote(here, arrived, z_sems, slot, up).wait_recv()
        add_into(here, arrived, 16)

    def z_pass(direction, kind, d):
        z_take(direction, kind, d)
        z_go(direction, kind, d - 1)

    compute(4)
    compute(3)
    have(4)
    z_go(1, 1, 4)
    compute(-3)
    have(3)
    z_go(0, 1, 3)
    y_take(4)
    z_go(0, 0, 4)
    compute(2)
    have(-3)
    compute(-2)
    y_take(-3)
    z_go(1, 0, 3)
    x_second(0)

    partial_sums[...] = jnp.zeros(partial_sums.shape, f32)

    @pl.loop(0, 8)
    def _(shard):
        at = shard_rows(shard)
        part = dot_nt(grad_qkv[...], weights[at, qkv_part]).astype(bf16)
        parts[1, shard] = part
        scaled = part.astype(f32) * gain[:, at]
        for q in range(share // 128):
            lanes = slice(q * 128, (q + 1) * 128)
            own = pl.ds(pl.multiple_of(shard * share + q * 128, 128), 128)
            centred = (rows[:, own].astype(f32) - row_mean[...]) * row_factor[...]
            partial_sums[0] += scaled[:, lanes]
            partial_sums[1] += scaled[:, lanes] * centred

    x_first(1)
    ones = jnp.ones((8, 128), f32)
    upper = lax.broadcasted_iota(jnp.int32, (8, tok), 0) < 4
    sums[...] = jnp.where(
        upper,
        exact_dot(ones, partial_sums[0], ((1,), (1,))),
        exact_dot(ones, partial_sums[1], ((1,), (1,))),
    )
    for o, peer in enumerate(peers):
        go(remote(sums, sums_got.at[o], s_sems, o, peer))

    have(2)
    have(-2)
    z_pass(1, 1, 4)
    y_take(3)
    z_pass(0, 0, 4)
    z_pass(0, 1, 3)
    y_take(-2)
    z_pass(1, 0, 3)
    compute(1)
    compute(-1)
    have(1)
    have(-1)
    x_third(0)
    z_pass(1, 1, 3)
    y_take(2)
    z_pass(0, 0, 3)
    compute(0)
    z_pass(0, 1, 2)
    y_take(-1)
    z_pass(1, 0, 2)
    have(0)
    x_second(1)
    z_pass(1, 1, 2)
    y_take(1)
    z_pass(0, 0, 2)
    l_take(0)

    @pl.loop(0, tok // step_rows)
    def _(i):
        at = pl.ds(pl.multiple_of(i * step_rows, step_rows), step_rows)
        total = parts[0, me_t, at, :].astype(f32) + l_got[0, at, :].astype(f32)
        attended[at, :] = jnp.where(live_rows(i, total.shape), total, 0.0).astype(bf16)

    x_third(1)
    total_sums = sums[...]
    for o, peer in enumerate(peers):
        remote(sums, sums_got.at[o], s_sems, o, peer).wait_recv()
        total_sums += sums_got[o]
    pick = lax.broadcasted_iota(jnp.int32, (8, 128), 0)
    partial_sums[0] = exact_dot(
        total_sums, jnp.where(pick == 0, 1.0 / model, 0.0).astype(f32), ((0,), (0,))
    )
    partial_sums[1] = exact_dot(
        total_sums, jnp.where(pick == 4, 1.0 / model, 0.0).astype(f32), ((0,), (0,))
    )
    z_take(0, 1, 1)
    z_take(1, 1, 1)
    go(remote(terms.at[z, 1 - yh, c, kept], y_got.at[kept], y_sems, 8, opposite))
    l_take(1)

    @pl.loop(0, tok // step_rows)
    def _(i):
        at = pl.ds(pl.multiple_of(i * step_rows, step_rows), step_rows)
        for q in range(share // 128):
            lanes = slice(q * 128, (q + 1) * 128)
            own = pl.ds(pl.multiple_of(me_t * share + q * 128, 128), 128)
            total = parts[1, me_t, at, lanes].astype(f32) + l_got[1, at, lanes].astype(f32)
            centred = (rows[at, own].astype(f32) - row_mean[at, :]) * row_factor[at, :]
            grad_rows[at, lanes] = (
                row_factor[at, :]
                * (total * gain[:, own] - partial_sums[0, at, :] - centred * partial_sums[1, at, :])
            ).astype(bf16)

    z_take(1, 0, 1)
    z_take(0, 0, 1)
    remote(terms.at[z, yh, c, crossing], y_got.at[crossing], y_sems, 7, opposite).wait_recv()
    remote(terms.at[z, yh, c, kept], y_got.at[kept], y_sems, 8, opposite).wait_recv()

    @pl.loop(0, depth // step_rows)
    def _(i):
        at = pl.ds(pl.multiple_of(i * step_rows, step_rows), step_rows)
        total = terms[z, yh, c, at, :].astype(f32) + y_got[at, :].astype(f32)
        grad_qkv_w[at, :] = total[:, :qkv_cols]
        grad_out_w[at, :] = total[:, qkv_cols:]

    for copy in sent:
        copy.wait_send()


def branch(bits, live, gain, qk_gain, patches, cotangent, qkv_weight, out_weight):
    bf16, f32 = jnp.bfloat16, jnp.float32
    tok, model = patches.shape
    qkv_cols, out_cols = qkv_weight.shape[1], out_weight.shape[1]
    wide = qkv_cols + out_cols
    depth = model // 32
    share = model // 8
    head_dim = qk_gain.shape[1]
    heads = out_cols // head_dim
    slots = live.shape[0]
    slot_rows = tok // slots
    hbm = pl.BlockSpec(memory_space=pl.ANY)
    vmem = pl.BlockSpec(memory_space=pltpu.VMEM)
    smem = pl.BlockSpec(memory_space=pltpu.SMEM)
    dma = pltpu.SemaphoreType.DMA
    sems = []
    for n in (5 * slots, 7 * slots, 45, 8, 14, 9, 12, 2, 7):
        sems += [dma((n,)), dma((n,))]
    return pl.pallas_call(
        branch_kernel,
        out_shape=(
            jax.ShapeDtypeStruct((tok, share), bf16),
            jax.ShapeDtypeStruct((tok, share), bf16),
            jax.ShapeDtypeStruct((depth, qkv_cols), f32),
            jax.ShapeDtypeStruct((depth, out_cols), f32),
        ),
        in_specs=[smem, smem, vmem, vmem, hbm, hbm, hbm, hbm],
        out_specs=(vmem,) * 4,
        scratch_shapes=[
            pltpu.VMEM((5, slots, slot_rows, share), bf16),
            pltpu.VMEM((5, slots, slot_rows, share), bf16),
            pltpu.VMEM((tok, model), bf16),
            pltpu.VMEM((model, wide), bf16),
            pltpu.VMEM((tok, model), bf16),
            pltpu.VMEM((tok, model), bf16),
            pltpu.VMEM((tok, 128), f32),
            pltpu.VMEM((tok, 128), f32),
            pltpu.VMEM((tok, qkv_cols), f32),
            pltpu.VMEM((heads, slots, slot_rows, slot_rows), f32),
            pltpu.VMEM((tok, out_cols), bf16),
            pltpu.VMEM((tok, out_cols), bf16),
            pltpu.VMEM((tok, qkv_cols), bf16),
            pltpu.VMEM((NZ, 2, 2, depth, wide), bf16),
            pltpu.VMEM((NZ, 2, depth, wide), bf16),
            pltpu.VMEM((7, depth - G_ROWS, wide), bf16),
            pltpu.VMEM((14, depth, wide), bf16),
            pltpu.VMEM((depth, wide), bf16),
            pltpu.VMEM((2, 8, tok, share), bf16),
            pltpu.VMEM((12, tok, share), bf16),
            pltpu.VMEM((2, tok, share), bf16),
            pltpu.VMEM((2, tok, 128), f32),
            pltpu.VMEM((8, tok), f32),
            pltpu.VMEM((7, 8, tok), f32),
        ]
        + sems
        + [dma((slots + 3,))],
        compiler_params=pltpu.CompilerParams(
            collective_id=0, has_side_effects=True, vmem_limit_bytes=60 * 2**20
        ),
        cost_estimate=pl.CostEstimate(
            flops=13 * 10**9, bytes_accessed=16 * 2**20, transcendentals=150528
        ),
    )(bits, live, gain, qk_gain, patches, cotangent, qkv_weight, out_weight)


def per_device(patches, cotangent, counts, masks, norm_gain, qk_gain, qkv_weight, out_weight):
    replicas = lax.axis_size("fsdp")
    my_replica = lax.axis_index("fsdp")
    bit = [jnp.bitwise_and(jnp.right_shift(masks, place), 1) for place in range(5)]
    bits = jnp.stack(
        [bit[1], bit[4], bit[3] ^ bit[4], bit[2] ^ bit[3], bit[0]], axis=1
    ).astype(jnp.int32)
    replica_ids = jnp.arange(replicas, dtype=jnp.int32)
    sources = jnp.bitwise_xor(my_replica, masks)
    run_counts = jnp.sum(jnp.where(replica_ids[:, None] == sources[None, :], counts, 0), axis=0)
    run_counts = run_counts.astype(jnp.int32)
    return branch(
        bits, run_counts, norm_gain[None, :], qk_gain, patches, cotangent, qkv_weight, out_weight
    )


def solution(mesh):
    in_specs = (
        P("fsdp", None),
        P("fsdp", None),
        P(),
        P(),
        P(),
        P(),
        P("fsdp", "tp"),
        P("fsdp", "tp"),
    )
    out_specs = (P("fsdp", "tp"), P("fsdp", "tp"), P("fsdp", "tp"), P("fsdp", "tp"))
    return jax.shard_map(
        per_device, mesh=mesh, in_specs=in_specs, out_specs=out_specs, check_vma=False
    )
```

time: 213 us -> 192 us (0.901)
  Pallas kernels: 193 us -> 180 us
  local copies, waits for them, and re-layouts: 16.1 us -> 8 us
    pallas_call x1 -> x0, Pallas kernels: 104 us -> none  [gather(): pl.pallas_call(gather_kernel, out_shape=(jax.ShapeDtypeStruct((tok, model...]
    pallas_call x1, Pallas kernels: 88.8 us -> 180 us  [branch(): pl.pallas_call(branch_kernel, out_shape=(jax.ShapeDtypeStruct((tok, share...]
    unnamed x16 -> x4, local copies, waits for them, and re-layouts: 15.6 us -> 6.87 us
where the time goes in v3:
time: 192 us; the launch traced here: 191 us
  Pallas kernels  180 us (94%)
  local copies, waits for them, and re-layouts  8 us (4%)
  other arithmetic  2.04 us (1%)
    pallas_call x1, Pallas kernels, branch(): pl.pallas_call(branch_kernel, out_shape=(jax.ShapeDtypeStruct((tok, share...  180 us
    unnamed x4, local copies, waits for them, and re-layouts  6.87 us

profile of v3, /device:TPU:2, one launch (start us, length us, event | category | flops | bytes accessed | tf_op | source)
XLA Modules:
  0.0 190.6 jit_solution(2512413886843586102)
XLA Ops:
  0.6 0.7 broadcast_xor_fusion
  1.3 1.4 select_reduce_fusion.live_ref
  2.7 0.1 copy.15
  2.8 0.1 copy.14
  2.9 0.1 copy.13
  2.9 0.1 copy.12
  3.0 0.1 copy.16
  3.1 0.7 stack.23.bits_ref
  3.8 179.9 %shard_map.111 = (bf16[448,384]{1,0:T(8,128)(2,1)}, bf16[448,384]{1,0:T(8,128)(2,1)}, f32[96,1152]{1,0:T(8,128)}, f32[96,384]{1,0:T(8,128)}) custom-call(s32[4,5]{1,0:T(4,128)} %stack.23.bits_ref, s32[4]{0:T(128)} %select_reduce_fusion.live_ref, f32[1,3072]{1,0:T(1,128)} %bitcast.11, f32[2,128]{1,0:T(2,128)} %qk_gain.1, bf16[448,3072]{1,0:T(8,128)(2,1)} %patches.1, ...), custom_call_target="tpu_custom_call" | custom-call | flops 12999999488 | bytes 16777216 | tf_op jit(solution)/shard_map/pallas_call | solution.py:687
  183.7 1.7 copy.21
  185.5 1.7 copy.22
  187.2 1.8 copy.23
  189.0 1.6 copy.24

commit v4 on v3

--- a/solution.py
+++ b/solution.py
@@ -9,7 +9,8 @@
 MESH = pl.DeviceIdType.MESH
 epsilon = 1e-06
 NZ, NX = 8, 4
-W_ROWS, G_ROWS = 32, 48
+SETTLE_PIECES = 2
+W_ROWS, G_ROWS = 48, 48
 
 
 def coords():
@@ -86,7 +87,7 @@
 
 
 def branch_kernel(
-    bits_ref, live_ref, gain, qk_gain, patches, cotangent, qkv_w, out_w,
+    masks_ref, counts_ref, gain, qk_gain, patches, cotangent, qkv_w, out_w,
     attended, grad_rows, grad_qkv_w, grad_out_w,
     hold, got, rows, weights, upstream, normed, row_mean, row_factor, projected, attention,
     mixed, grad_mixed, grad_qkv, terms, theirs, y_part, z_got, y_got, parts, x_got, l_got,
@@ -121,6 +122,19 @@
     peers = [(my_f, lax.rem(me_t + o, 8)) for o in range(1, 8)]
     f32, bf16 = jnp.float32, jnp.bfloat16
 
+    def live_count(k):
+        return counts_ref[k, jnp.bitwise_xor(my_f, masks_ref[k])]
+
+    def mask_bit(k, place):
+        return jnp.bitwise_and(lax.shift_right_logical(masks_ref[k], place), 1)
+
+    def takes(k, step):
+        which = -1 if step == 0 else order[k][step - 1]
+        if which in (-1, 7, 0):
+            return mask_bit(k, {-1: 1, 7: 4, 0: 0}[which]) > 0
+        places = (3, 4) if which == 3 else (2, 3)
+        return mask_bit(k, places[0]) != mask_bit(k, places[1])
+
     def slot_at(s):
         return pl.ds(s * slot_rows, slot_rows)
 
@@ -202,23 +216,22 @@
         slot = w_index((w_route(direction), (there, kind, first, count)))
         go(remote(view, view, c_sems, slot, up if direction == 0 else down))
 
-    def w_take(direction, kind, d):
-        signed = -d if direction == 0 else d
-        piece = (signed, kind) + w_rows(kind)
-        w_copy(w_route(direction), piece, up).wait_recv()
-        if d < limits[direction, kind]:
-            w_send(direction, kind, d)
-        if kind == 0:
-            owner = z_at(signed) * 4 + yh * 2 + c
-            view = weight_at(owner, *rest)
-            go(remote(view, view, c_sems, w_index(("y", (signed, 1) + rest)), opposite))
-        w_core(piece)
-
-    def w_round(d):
-        for kind in range(2):
-            for direction in range(2):
-                if d <= limits[direction, kind]:
-                    w_take(direction, kind, d)
+    def w_take(kind, d):
+        for direction in range(2):
+            if d <= limits[direction, kind]:
+                signed = -d if direction == 0 else d
+                piece = (signed, kind) + w_rows(kind)
+                w_copy(w_route(direction), piece, up).wait_recv()
+                if kind == 0:
+                    owner = z_at(signed) * 4 + yh * 2 + c
+                    view = weight_at(owner, *rest)
+                    go(remote(view, view, c_sems, w_index(("y", (signed, 1) + rest)), opposite))
+                w_core(piece)
+
+    def w_pass(kind, d):
+        for direction in range(2):
+            if d < limits[direction, kind]:
+                w_send(direction, kind, d)
 
     def w_across(signed):
         piece = (signed, 1) + rest
@@ -230,25 +243,20 @@
     for copy in own_w:
         copy.wait()
     whole = (0, depth)
-    view = weight_at(my_f, *whole)
-    go(remote(view, view, c_sems, w_index(("y", (0, 1) + whole)), opposite))
-    w_core((0, 0) + whole)
-    w_send(0, 0, 0)
-    w_send(1, 0, 0)
+    w_pass(0, 0)
     for copy in own:
         copy.wait()
 
     partner = {3: z3, 7: z7, 1: z1, 0: sibling}
-    bit_column = {7: 1, 3: 2, 1: 3, 0: 4}
     order = [[7, 3, 1, 0], [3, 7, 1, 0], [7, 3, 1, 0], [3, 7, 1, 0]]
 
     def merge(k, step):
         remote(got.at[step, k], got.at[step, k], a_sems, step * slots + k, sibling).wait_recv()
-        taken = bits_ref[k, 0 if step == 0 else bit_column[order[k][step - 1]]] > 0
+        taken = takes(k, step)
         return lax.select_n(taken, hold[step, k], got[step, k])
 
-    def row_step(step):
-        for k in range(slots):
+    def row_step(step, which_slots=(0, 1, 2, 3)):
+        for k in which_slots:
             hold[step + 1, k] = merge(k, step)
             go(
                 remote(
@@ -264,7 +272,7 @@
     def rows_first(k):
         merged = merge(k, 4).astype(f32)
         place = lax.broadcasted_iota(jnp.int32, (slot_rows, share), 0)
-        live = place < live_ref[k]
+        live = place < live_count(k)
         rows[slot_at(k), columns(me_t)] = jnp.where(live, merged, 0.0).astype(bf16)
         go(row_copy(k, x, yl, 0, beside))
         go(row_copy(k, x, yl, 1, right))
@@ -318,29 +326,60 @@
 
     def live_rows(i, shape):
         place = lax.broadcasted_iota(jnp.int32, shape, 0) + lax.rem(i, per_slot) * step_rows
-        return place < live_ref[lax.div(i, per_slot)]
-
-    row_step(0)
+        return place < live_count(lax.div(i, per_slot))
+
+    row_step(0, (0, 1, 2, 3))
+    view = weight_at(my_f, *whole)
+    go(remote(view, view, c_sems, w_index(("y", (0, 1) + whole)), opposite))
+    w_core((0, 0) + whole)
+    w_take(0, 1)
+    row_step(1, (0, 1, 2, 3))
     w_copy("y", (0, 1) + whole, opposite).wait_recv()
-    w_send(0, 1, 0)
-    w_send(1, 1, 0)
     w_core((0, 1) + whole)
-    row_step(1)
-    w_round(1)
-    row_step(2)
+    row_step(2, (0, 1, 2, 3))
+    w_pass(0, 1)
+    w_pass(1, 0)
     w_across(-1)
     w_across(1)
-    row_step(3)
-    w_round(2)
-    for k in range(slots):
-        rows_first(k)
-    for k in range(slots):
-        rows_second(k)
+    row_step(3, (0, 1, 2, 3))
+    rows_first(0)
+    rows_first(1)
+    rows_first(2)
+    rows_first(3)
+    w_take(0, 2)
+    w_pass(0, 2)
+    rows_second(0)
+    rows_second(1)
+    rows_second(2)
+    rows_second(3)
+    w_take(1, 1)
+    w_pass(1, 1)
+    rows_third(0)
+    rows_third(1)
+    rows_third(2)
+    rows_third(3)
     w_across(-2)
     w_across(2)
-    for k in range(slots):
-        rows_third(k)
-    w_round(3)
+    w_take(0, 3)
+    w_pass(0, 3)
+    w_take(1, 2)
+    w_pass(1, 2)
+    rows_last(0)
+    norm_slot(0)
+    rows_last(1)
+    norm_slot(1)
+    w_across(-3)
+    w_across(3)
+    rows_last(2)
+    norm_slot(2)
+    rows_last(3)
+    norm_slot(3)
+    w_take(0, 4)
+    w_take(1, 3)
+    w_pass(1, 3)
+    project(0)
+    project(-1)
+    project(1)
     load.wait()
 
     @pl.loop(0, tok // step_rows)
@@ -348,21 +387,12 @@
         at = pl.ds(pl.multiple_of(i * step_rows, step_rows), step_rows)
         values = upstream[at, :].astype(f32)
         upstream[at, :] = jnp.where(live_rows(i, values.shape), values, 0.0).astype(bf16)
-
-    for k in range(slots):
-        rows_last(k)
-        norm_slot(k)
-    project(0)
-    project(-1)
-    project(1)
-    w_across(-3)
-    w_across(3)
     project(-2)
     project(2)
-    w_round(4)
+    w_take(1, 4)
+    w_across(-4)
     project(-3)
     project(3)
-    w_across(-4)
     project(4)
 
     query_scale = qk_gain[0:1, :] * head_dim ** (-0.5)
@@ -390,7 +420,7 @@
         j = lax.broadcasted_iota(jnp.int32, (slot_rows, slot_rows), 1)
         for s in range(slots):
             (_, _, query), (_, _, key_rows), values = head_rows(h, s)
-            count = live_ref[s]
+            count = live_count(s)
             allowed = (jnp.maximum(i, j) < count) | (i == j)
             raised = jnp.where(allowed, jnp.exp(dot_nt(query, key_rows)), 0.0)
             weight = raised / jnp.sum(raised, axis=-1, keepdims=True)
@@ -425,22 +455,23 @@
         add_into(parts.at[p, shard], x_got.at[slot])
 
     def x_first(p):
-        for d in (2, 1):
-            for kind in (1, 0):
-                for direction in range(2):
-                    if d == x_limits[direction, kind]:
-                        x_go(p, direction, kind, d)
+        x_go(p, 0, 0, 2)
+        x_go(p, 1, 1, 2)
 
     def x_second(p):
         x_take(p, 1, 1, 2)
         x_go(p, 1, 1, 1)
+        x_go(p, 0, 1, 1)
         x_take(p, 0, 0, 2)
-        x_go(p, 0, 0, 1)
 
     def x_third(p):
         x_take(p, 0, 1, 1)
         x_take(p, 1, 1, 1)
         go(remote(parts.at[p, x * 2 + 1 - yl], l_got.at[p], l_sems, p, beside))
+        x_go(p, 0, 0, 1)
+        x_go(p, 1, 0, 1)
+
+    def x_last(p):
         x_take(p, 1, 0, 1)
         x_take(p, 0, 0, 1)
 
@@ -503,13 +534,18 @@
         )
 
     def have(distance):
+        zz = z_at(distance)
+        remote(
+            terms.at[zz, :, c], theirs.at[zz], core_sems, distances.index(distance), sibling
+        ).wait_recv()
+        for y in range(2):
+            add_into(terms.at[zz, y, c], theirs.at[zz, y])
+
+    def y_go(distance):
         i = distances.index(distance)
         zz = z_at(distance)
-        remote(terms.at[zz, :, c], theirs.at[zz], core_sems, i, sibling).wait_recv()
-        add_into(terms.at[zz, 1 - yh, c], theirs.at[zz, 1 - yh])
         target = y_got.at[crossing] if distance == 0 else y_part.at[i]
         go(remote(terms.at[zz, 1 - yh, c, crossing], target, y_sems, i, opposite))
-        add_into(terms.at[zz, yh, c], theirs.at[zz, yh])
 
     def y_take(distance):
         i = distances.index(distance)
@@ -546,21 +582,26 @@
         z_go(direction, kind, d - 1)
 
     compute(4)
+    compute(-3)
+    have(4)
+    y_go(4)
+    z_go(1, 1, 4)
+    have(-3)
+    y_go(-3)
     compute(3)
-    have(4)
-    z_go(1, 1, 4)
-    compute(-3)
     have(3)
     z_go(0, 1, 3)
+    x_second(0)
+    compute(2)
+    have(2)
+    compute(-2)
+    have(-2)
     y_take(4)
     z_go(0, 0, 4)
-    compute(2)
-    have(-3)
-    compute(-2)
+    y_go(3)
     y_take(-3)
     z_go(1, 0, 3)
-    x_second(0)
-
+    y_go(-2)
     partial_sums[...] = jnp.zeros(partial_sums.shape, f32)
 
     @pl.loop(0, 8)
@@ -575,7 +616,6 @@
             centred = (rows[:, own].astype(f32) - row_mean[...]) * row_factor[...]
             partial_sums[0] += scaled[:, lanes]
             partial_sums[1] += scaled[:, lanes] * centred
-
     x_first(1)
     ones = jnp.ones((8, 128), f32)
     upper = lax.broadcasted_iota(jnp.int32, (8, tok), 0) < 4
@@ -586,32 +626,31 @@
     )
     for o, peer in enumerate(peers):
         go(remote(sums, sums_got.at[o], s_sems, o, peer))
-
-    have(2)
-    have(-2)
     z_pass(1, 1, 4)
+    z_pass(0, 1, 3)
+    x_third(0)
+    compute(1)
+    have(1)
+    compute(-1)
+    have(-1)
     y_take(3)
     z_pass(0, 0, 4)
-    z_pass(0, 1, 3)
+    y_go(2)
     y_take(-2)
     z_pass(1, 0, 3)
-    compute(1)
-    compute(-1)
-    have(1)
-    have(-1)
-    x_third(0)
+    y_go(-1)
+    compute(0)
+    have(0)
+    x_second(1)
     z_pass(1, 1, 3)
+    z_pass(0, 1, 2)
     y_take(2)
     z_pass(0, 0, 3)
-    compute(0)
-    z_pass(0, 1, 2)
+    y_go(1)
     y_take(-1)
     z_pass(1, 0, 2)
-    have(0)
-    x_second(1)
-    z_pass(1, 1, 2)
-    y_take(1)
-    z_pass(0, 0, 2)
+    y_go(0)
+    x_last(0)
     l_take(0)
 
     @pl.loop(0, tok // step_rows)
@@ -619,8 +658,13 @@
         at = pl.ds(pl.multiple_of(i * step_rows, step_rows), step_rows)
         total = parts[0, me_t, at, :].astype(f32) + l_got[0, at, :].astype(f32)
         attended[at, :] = jnp.where(live_rows(i, total.shape), total, 0.0).astype(bf16)
-
+    z_pass(1, 1, 2)
+    y_take(1)
+    z_pass(0, 0, 2)
     x_third(1)
+    z_take(0, 1, 1)
+    z_take(1, 1, 1)
+    go(remote(terms.at[z, 1 - yh, c, kept], y_got.at[kept], y_sems, 8, opposite))
     total_sums = sums[...]
     for o, peer in enumerate(peers):
         remote(sums, sums_got.at[o], s_sems, o, peer).wait_recv()
@@ -632,9 +676,7 @@
     partial_sums[1] = exact_dot(
         total_sums, jnp.where(pick == 4, 1.0 / model, 0.0).astype(f32), ((0,), (0,))
     )
-    z_take(0, 1, 1)
-    z_take(1, 1, 1)
-    go(remote(terms.at[z, 1 - yh, c, kept], y_got.at[kept], y_sems, 8, opposite))
+    x_last(1)
     l_take(1)
 
     @pl.loop(0, tok // step_rows)
@@ -649,7 +691,6 @@
                 row_factor[at, :]
                 * (total * gain[:, own] - partial_sums[0, at, :] - centred * partial_sums[1, at, :])
             ).astype(bf16)
-
     z_take(1, 0, 1)
     z_take(0, 0, 1)
     remote(terms.at[z, yh, c, crossing], y_got.at[crossing], y_sems, 7, opposite).wait_recv()
@@ -666,7 +707,7 @@
         copy.wait_send()
 
 
-def branch(bits, live, gain, qk_gain, patches, cotangent, qkv_weight, out_weight):
+def branch(masks, counts, gain, qk_gain, patches, cotangent, qkv_weight, out_weight):
     bf16, f32 = jnp.bfloat16, jnp.float32
     tok, model = patches.shape
     qkv_cols, out_cols = qkv_weight.shape[1], out_weight.shape[1]
@@ -675,7 +716,7 @@
     share = model // 8
     head_dim = qk_gain.shape[1]
     heads = out_cols // head_dim
-    slots = live.shape[0]
+    slots = masks.shape[0]
     slot_rows = tok // slots
     hbm = pl.BlockSpec(memory_space=pl.ANY)
     vmem = pl.BlockSpec(memory_space=pltpu.VMEM)
@@ -728,22 +769,43 @@
         cost_estimate=pl.CostEstimate(
             flops=13 * 10**9, bytes_accessed=16 * 2**20, transcendentals=150528
         ),
-    )(bits, live, gain, qk_gain, patches, cotangent, qkv_weight, out_weight)
+    )(masks, counts, gain, qk_gain, patches, cotangent, qkv_weight, out_weight)
+
+
+def settle_kernel(*refs):
+    sem = refs[-1]
+    half = len(refs) // 2
+    copies = []
+    for source, target in zip(refs[:half], refs[half:-1]):
+        part = source.shape[0] // SETTLE_PIECES
+        for i in range(SETTLE_PIECES):
+            at = pl.ds(i * part, part)
+            copies.append(
+                pltpu.make_async_copy(source.at[at], target.at[at], sem.at[len(copies)])
+            )
+    for copy in copies:
+        copy.start()
+    for copy in copies:
+        copy.wait()
+
+
+def settle(arrays):
+    hbm = pl.BlockSpec(memory_space=pltpu.HBM)
+    return pl.pallas_call(
+        settle_kernel,
+        out_shape=tuple(jax.ShapeDtypeStruct(a.shape, a.dtype) for a in arrays),
+        in_specs=[hbm] * len(arrays),
+        out_specs=(hbm,) * len(arrays),
+        scratch_shapes=[pltpu.SemaphoreType.DMA((SETTLE_PIECES * len(arrays),))],
+        compiler_params=pltpu.CompilerParams(vmem_limit_bytes=60 * 2**20),
+    )(*arrays)
 
 
 def per_device(patches, cotangent, counts, masks, norm_gain, qk_gain, qkv_weight, out_weight):
-    replicas = lax.axis_size("fsdp")
-    my_replica = lax.axis_index("fsdp")
-    bit = [jnp.bitwise_and(jnp.right_shift(masks, place), 1) for place in range(5)]
-    bits = jnp.stack(
-        [bit[1], bit[4], bit[3] ^ bit[4], bit[2] ^ bit[3], bit[0]], axis=1
-    ).astype(jnp.int32)
-    replica_ids = jnp.arange(replicas, dtype=jnp.int32)
-    sources = jnp.bitwise_xor(my_replica, masks)
-    run_counts = jnp.sum(jnp.where(replica_ids[:, None] == sources[None, :], counts, 0), axis=0)
-    run_counts = run_counts.astype(jnp.int32)
-    return branch(
-        bits, run_counts, norm_gain[None, :], qk_gain, patches, cotangent, qkv_weight, out_weight
+    return settle(
+        branch(
+            masks, counts.T, norm_gain[None, :], qk_gain, patches, cotangent, qkv_weight, out_weight
+        )
     )
 
 

time: 192 us -> 193 us (level)
  Pallas kernels: 180 us -> 191 us
  local copies, waits for them, and re-layouts: 8 us -> 0 us
  other arithmetic: 2.04 us -> 0 us
    pallas_call x0 -> x1, Pallas kernels: none -> 39.9 us  [settle(): pl.pallas_call(settle_kernel, out_shape=tuple((jax.ShapeDtypeStruct(a.sha...]
    pallas_call x1, Pallas kernels: 180 us -> 152 us  [branch(): pl.pallas_call(branch_kernel, out_shape=(jax.ShapeDtypeStruct((tok, share...]
    unnamed x4 -> x0, local copies, waits for them, and re-layouts: 6.87 us -> none
where the time goes in v4:
time: 193 us; the launch traced here: 192 us
  Pallas kernels  191 us (99%)
    pallas_call x1, Pallas kernels, branch(): pl.pallas_call(branch_kernel, out_shape=(jax.ShapeDtypeStruct((tok, share...  152 us
    pallas_call x1, Pallas kernels, settle(): pl.pallas_call(settle_kernel, out_shape=tuple((jax.ShapeDtypeStruct(a.sha...  39.9 us

profile of v4, /device:TPU:2, one launch (start us, length us, event | category | flops | bytes accessed | tf_op | source)
XLA Modules:
  0.0 192.2 jit_solution(15215416216747026065)
XLA Ops:
  0.6 151.5 %shard_map.111 = (bf16[448,384]{1,0:T(8,128)(2,1)}, bf16[448,384]{1,0:T(8,128)(2,1)}, f32[96,1152]{1,0:T(8,128)}, f32[96,384]{1,0:T(8,128)}) custom-call(s32[4]{0:T(128)} %masks_ref.1, s32[4,32]{1,0:T(4,128)} %bitcast.3, f32[1,3072]{1,0:T(1,128)} %bitcast.2, f32[2,128]{1,0:T(2,128)} %qk_gain.1, bf16[448,3072]{1,0:T(8,128)(2,1)} %patches.1, ...), custom_call_target="tpu_custom_call" | custom-call | flops 12999999488 | bytes 16777216 | tf_op jit(solution)/shard_map/pallas_call | solution.py:728
  152.2 39.9 %shard_map.112 = (bf16[448,384]{1,0:T(8,128)(2,1)}, bf16[448,384]{1,0:T(8,128)(2,1)}, f32[96,1152]{1,0:T(8,128)}, f32[96,384]{1,0:T(8,128)}) custom-call(bf16[448,384]{1,0:T(8,128)(2,1)} %get-tuple-element.8.refs_0_, bf16[448,384]{1,0:T(8,128)(2,1)} %get-tuple-element.9.refs_1_, f32[96,1152]{1,0:T(8,128)} %get-tuple-element.10.refs_2_, ...), custom_call_target="tpu_custom_call" | custom-call | tf_op jit(solution)/shard_map/pallas_call | solution.py:794

commit v5 on v4

--- a/solution.py
+++ b/solution.py
@@ -9,7 +9,6 @@
 MESH = pl.DeviceIdType.MESH
 epsilon = 1e-06
 NZ, NX = 8, 4
-SETTLE_PIECES = 2
 W_ROWS, G_ROWS = 48, 48
 
 
@@ -773,19 +772,20 @@
 
 
 def settle_kernel(*refs):
+    n = len(refs) // 3
     sem = refs[-1]
-    half = len(refs) // 2
-    copies = []
-    for source, target in zip(refs[:half], refs[half:-1]):
-        part = source.shape[0] // SETTLE_PIECES
-        for i in range(SETTLE_PIECES):
-            at = pl.ds(i * part, part)
-            copies.append(
-                pltpu.make_async_copy(source.at[at], target.at[at], sem.at[len(copies)])
-            )
-    for copy in copies:
+    arrive = [
+        pltpu.make_async_copy(refs[i], refs[2 * n + i], sem.at[i]) for i in range(n)
+    ]
+    leave = [
+        pltpu.make_async_copy(refs[2 * n + i], refs[n + i], sem.at[n + i]) for i in range(n)
+    ]
+    for copy in arrive:
         copy.start()
-    for copy in copies:
+    for one, other in zip(arrive, leave):
+        one.wait()
+        other.start()
+    for copy in leave:
         copy.wait()
 
 
@@ -796,7 +796,8 @@
         out_shape=tuple(jax.ShapeDtypeStruct(a.shape, a.dtype) for a in arrays),
         in_specs=[hbm] * len(arrays),
         out_specs=(hbm,) * len(arrays),
-        scratch_shapes=[pltpu.SemaphoreType.DMA((SETTLE_PIECES * len(arrays),))],
+        scratch_shapes=[pltpu.VMEM(a.shape, a.dtype) for a in arrays]
+        + [pltpu.SemaphoreType.DMA((2 * len(arrays),))],
         compiler_params=pltpu.CompilerParams(vmem_limit_bytes=60 * 2**20),
     )(*arrays)
 

time: 193 us -> 155 us (0.80)
  Pallas kernels: 191 us -> 154 us
    pallas_call x1, Pallas kernels: 39.9 us -> 2.1 us  [settle(): pl.pallas_call(settle_kernel, out_shape=tuple((jax.ShapeDtypeStruct(a.sha...]
where the time goes in v5:
time: 155 us; the launch traced here: 154 us
  Pallas kernels  154 us (99%)
    pallas_call x1, Pallas kernels, branch(): pl.pallas_call(branch_kernel, out_shape=(jax.ShapeDtypeStruct((tok, share...  152 us

profile of v5, /device:TPU:2, one launch (start us, length us, event | category | flops | bytes accessed | tf_op | source)
XLA Modules:
  0.0 154.4 jit_solution(10517737546017398391)
XLA Ops:
  0.6 151.5 %shard_map.111 = (bf16[448,384]{1,0:T(8,128)(2,1)}, bf16[448,384]{1,0:T(8,128)(2,1)}, f32[96,1152]{1,0:T(8,128)}, f32[96,384]{1,0:T(8,128)}) custom-call(s32[4]{0:T(128)} %masks_ref.1, s32[4,32]{1,0:T(4,128)} %bitcast.3, f32[1,3072]{1,0:T(1,128)} %bitcast.2, f32[2,128]{1,0:T(2,128)} %qk_gain.1, bf16[448,3072]{1,0:T(8,128)(2,1)} %patches.1, ...), custom_call_target="tpu_custom_call" | custom-call | flops 12999999488 | bytes 16777216 | tf_op jit(solution)/shard_map/pallas_call | solution.py:727
  152.2 2.1 %shard_map.112 = (bf16[448,384]{1,0:T(8,128)(2,1)}, bf16[448,384]{1,0:T(8,128)(2,1)}, f32[96,1152]{1,0:T(8,128)}, f32[96,384]{1,0:T(8,128)}) custom-call(bf16[448,384]{1,0:T(8,128)(2,1)} %get-tuple-element.8.refs_0_, bf16[448,384]{1,0:T(8,128)(2,1)} %get-tuple-element.9.refs_1_, f32[96,1152]{1,0:T(8,128)} %get-tuple-element.10.refs_2_, ...), custom_call_target="tpu_custom_call" | custom-call | tf_op jit(solution)/shard_map/pallas_call | solution.py:794

commit v6 on v5

--- a/solution.py
+++ b/solution.py
@@ -77,7 +77,7 @@
 
 
 def add_into(total, other, rows_at=32):
-    @pl.loop(0, total.shape[0] // rows_at)
+    @pl.loop(0, total.shape[0] // rows_at, unroll=True)
     def _(i):
         at = pl.ds(pl.multiple_of(i * rows_at, rows_at), rows_at)
         total[at, :] = (
@@ -242,7 +242,6 @@
     for copy in own_w:
         copy.wait()
     whole = (0, depth)
-    w_pass(0, 0)
     for copy in own:
         copy.wait()
 
@@ -295,7 +294,7 @@
         row_copy(k, lax.rem(x + 2, NX), 1 - yl, 6, left).wait_recv()
 
     def norm_slot(k):
-        @pl.loop(0, per_slot)
+        @pl.loop(0, per_slot, unroll=True)
         def _(i):
             at = pl.ds(pl.multiple_of(k * slot_rows + i * step_rows, step_rows), step_rows)
             values = rows[at, :].astype(f32)
@@ -327,12 +326,20 @@
         place = lax.broadcasted_iota(jnp.int32, shape, 0) + lax.rem(i, per_slot) * step_rows
         return place < live_count(lax.div(i, per_slot))
 
+    w_pass(0, 0)
     row_step(0, (0, 1, 2, 3))
     view = weight_at(my_f, *whole)
     go(remote(view, view, c_sems, w_index(("y", (0, 1) + whole)), opposite))
     w_core((0, 0) + whole)
     w_take(0, 1)
     row_step(1, (0, 1, 2, 3))
+    load.wait()
+
+    @pl.loop(0, tok // step_rows)
+    def _(i):
+        at = pl.ds(pl.multiple_of(i * step_rows, step_rows), step_rows)
+        values = upstream[at, :].astype(f32)
+        upstream[at, :] = jnp.where(live_rows(i, values.shape), values, 0.0).astype(bf16)
     w_copy("y", (0, 1) + whole, opposite).wait_recv()
     w_core((0, 1) + whole)
     row_step(2, (0, 1, 2, 3))
@@ -379,13 +386,6 @@
     project(0)
     project(-1)
     project(1)
-    load.wait()
-
-    @pl.loop(0, tok // step_rows)
-    def _(i):
-        at = pl.ds(pl.multiple_of(i * step_rows, step_rows), step_rows)
-        values = upstream[at, :].astype(f32)
-        upstream[at, :] = jnp.where(live_rows(i, values.shape), values, 0.0).astype(bf16)
     project(-2)
     project(2)
     w_take(1, 4)
@@ -413,7 +413,7 @@
             values,
         )
 
-    @pl.loop(0, heads)
+    @pl.loop(0, heads, unroll=True)
     def _(h):
         i = lax.broadcasted_iota(jnp.int32, (slot_rows, slot_rows), 0)
         j = lax.broadcasted_iota(jnp.int32, (slot_rows, slot_rows), 1)
@@ -480,7 +480,7 @@
     def shard_rows(shard):
         return pl.ds(pl.multiple_of(shard * share, share), share)
 
-    @pl.loop(0, 8)
+    @pl.loop(0, 8, unroll=2)
     def _(shard):
         parts[0, shard] = dot_nt(mixed[...], weights[shard_rows(shard), out_part]).astype(bf16)
 
@@ -488,7 +488,7 @@
 
     grad_mixed[...] = dot_nn(upstream[...], weights[:, out_part]).astype(bf16)
 
-    @pl.loop(0, heads)
+    @pl.loop(0, heads, unroll=True)
     def _(h):
         for s in range(slots):
             (query_hat, query_factor, query), (key_hat, key_factor, key_rows), values = head_rows(
@@ -580,42 +580,73 @@
         z_take(direction, kind, d)
         z_go(direction, kind, d - 1)
 
+    partial_sums[...] = jnp.zeros(partial_sums.shape, f32)
+
+    def back_part(distance):
+        @pl.loop(0, 2, unroll=True)
+        def _(low):
+            shard = lax.rem(x + distance, NX) * 2 + low
+            at = shard_rows(shard)
+            part = dot_nt(grad_qkv[...], weights[at, qkv_part]).astype(bf16)
+            parts[1, shard] = part
+            scaled = part.astype(f32) * gain[:, at]
+            for q in range(share // 128):
+                lanes = slice(q * 128, (q + 1) * 128)
+                own = pl.ds(pl.multiple_of(shard * share + q * 128, 128), 128)
+                centred = (rows[:, own].astype(f32) - row_mean[...]) * row_factor[...]
+                partial_sums[0] += scaled[:, lanes]
+                partial_sums[1] += scaled[:, lanes] * centred
     compute(4)
     compute(-3)
+    compute(3)
+    x_second(0)
     have(4)
     y_go(4)
+    compute(2)
+    have(-3)
+    have(3)
+    back_part(2)
     z_go(1, 1, 4)
-    have(-3)
+    z_go(0, 1, 3)
     y_go(-3)
-    compute(3)
-    have(3)
-    z_go(0, 1, 3)
-    x_second(0)
-    compute(2)
+    x_first(1)
+    back_part(1)
     have(2)
-    compute(-2)
-    have(-2)
+    y_go(2)
     y_take(4)
     z_go(0, 0, 4)
+    compute(-2)
+    z_pass(0, 1, 3)
+    compute(1)
+    y_take(-3)
+    z_pass(1, 1, 4)
     y_go(3)
-    y_take(-3)
+    back_part(0)
+    x_third(0)
     z_go(1, 0, 3)
+    have(-2)
+    compute(0)
+    back_part(3)
+    y_take(3)
+    have(0)
     y_go(-2)
-    partial_sums[...] = jnp.zeros(partial_sums.shape, f32)
-
-    @pl.loop(0, 8)
-    def _(shard):
-        at = shard_rows(shard)
-        part = dot_nt(grad_qkv[...], weights[at, qkv_part]).astype(bf16)
-        parts[1, shard] = part
-        scaled = part.astype(f32) * gain[:, at]
-        for q in range(share // 128):
-            lanes = slice(q * 128, (q + 1) * 128)
-            own = pl.ds(pl.multiple_of(shard * share + q * 128, 128), 128)
-            centred = (rows[:, own].astype(f32) - row_mean[...]) * row_factor[...]
-            partial_sums[0] += scaled[:, lanes]
-            partial_sums[1] += scaled[:, lanes] * centred
-    x_first(1)
+    z_pass(0, 0, 4)
+    have(1)
+    z_pass(0, 1, 2)
+    z_pass(1, 1, 3)
+    x_second(1)
+    compute(-1)
+    have(-1)
+    y_go(1)
+    y_go(-1)
+    z_pass(1, 1, 2)
+    z_take(1, 1, 1)
+    z_take(0, 1, 1)
+    y_take(2)
+    z_pass(0, 0, 3)
+    y_take(-2)
+    z_pass(1, 0, 3)
+    x_third(1)
     ones = jnp.ones((8, 128), f32)
     upper = lax.broadcasted_iota(jnp.int32, (8, tok), 0) < 4
     sums[...] = jnp.where(
@@ -625,45 +656,8 @@
     )
     for o, peer in enumerate(peers):
         go(remote(sums, sums_got.at[o], s_sems, o, peer))
-    z_pass(1, 1, 4)
-    z_pass(0, 1, 3)
-    x_third(0)
-    compute(1)
-    have(1)
-    compute(-1)
-    have(-1)
-    y_take(3)
-    z_pass(0, 0, 4)
-    y_go(2)
-    y_take(-2)
-    z_pass(1, 0, 3)
-    y_go(-1)
-    compute(0)
-    have(0)
-    x_second(1)
-    z_pass(1, 1, 3)
-    z_pass(0, 1, 2)
-    y_take(2)
-    z_pass(0, 0, 3)
-    y_go(1)
-    y_take(-1)
-    z_pass(1, 0, 2)
-    y_go(0)
+    y_take(1)
     x_last(0)
-    l_take(0)
-
-    @pl.loop(0, tok // step_rows)
-    def _(i):
-        at = pl.ds(pl.multiple_of(i * step_rows, step_rows), step_rows)
-        total = parts[0, me_t, at, :].astype(f32) + l_got[0, at, :].astype(f32)
-        attended[at, :] = jnp.where(live_rows(i, total.shape), total, 0.0).astype(bf16)
-    z_pass(1, 1, 2)
-    y_take(1)
-    z_pass(0, 0, 2)
-    x_third(1)
-    z_take(0, 1, 1)
-    z_take(1, 1, 1)
-    go(remote(terms.at[z, 1 - yh, c, kept], y_got.at[kept], y_sems, 8, opposite))
     total_sums = sums[...]
     for o, peer in enumerate(peers):
         remote(sums, sums_got.at[o], s_sems, o, peer).wait_recv()
@@ -675,7 +669,19 @@
     partial_sums[1] = exact_dot(
         total_sums, jnp.where(pick == 4, 1.0 / model, 0.0).astype(f32), ((0,), (0,))
     )
+    y_take(-1)
+    l_take(0)
+
+    @pl.loop(0, tok // step_rows)
+    def _(i):
+        at = pl.ds(pl.multiple_of(i * step_rows, step_rows), step_rows)
+        total = parts[0, me_t, at, :].astype(f32) + l_got[0, at, :].astype(f32)
+        attended[at, :] = jnp.where(live_rows(i, total.shape), total, 0.0).astype(bf16)
+    z_pass(0, 0, 2)
+    go(remote(terms.at[z, 1 - yh, c, kept], y_got.at[kept], y_sems, 8, opposite))
+    z_pass(1, 0, 2)
     x_last(1)
+    y_go(0)
     l_take(1)
 
     @pl.loop(0, tok // step_rows)
@@ -690,8 +696,8 @@
                 row_factor[at, :]
                 * (total * gain[:, own] - partial_sums[0, at, :] - centred * partial_sums[1, at, :])
             ).astype(bf16)
+    z_take(0, 0, 1)
     z_take(1, 0, 1)
-    z_take(0, 0, 1)
     remote(terms.at[z, yh, c, crossing], y_got.at[crossing], y_sems, 7, opposite).wait_recv()
     remote(terms.at[z, yh, c, kept], y_got.at[kept], y_sems, 8, opposite).wait_recv()
 

time: 155 us -> 146 us (0.942)
  Pallas kernels: 154 us -> 144 us
    pallas_call x1, Pallas kernels: 152 us -> 142 us  [branch(): pl.pallas_call(branch_kernel, out_shape=(jax.ShapeDtypeStruct((tok, share...]
where the time goes in v6:
time: 146 us; the launch traced here: 145 us
  Pallas kernels  144 us (99%)
    pallas_call x1, Pallas kernels, branch(): pl.pallas_call(branch_kernel, out_shape=(jax.ShapeDtypeStruct((tok, share...  142 us

profile of v6, /device:TPU:2, one launch (start us, length us, event | category | flops | bytes accessed | tf_op | source)
XLA Modules:
  0.0 145.1 jit_solution(17853462647092818678)
XLA Ops:
  0.6 142.1 %shard_map.111 = (bf16[448,384]{1,0:T(8,128)(2,1)}, bf16[448,384]{1,0:T(8,128)(2,1)}, f32[96,1152]{1,0:T(8,128)}, f32[96,384]{1,0:T(8,128)}) custom-call(s32[4]{0:T(128)} %masks_ref.1, s32[4,32]{1,0:T(4,128)} %bitcast.3, f32[1,3072]{1,0:T(1,128)} %bitcast.2, f32[2,128]{1,0:T(2,128)} %qk_gain.1, bf16[448,3072]{1,0:T(8,128)(2,1)} %patches.1, ...), custom_call_target="tpu_custom_call" | custom-call | flops 12999999488 | bytes 16777216 | tf_op jit(solution)/shard_map/pallas_call | solution.py:733
  142.8 2.1 %shard_map.112 = (bf16[448,384]{1,0:T(8,128)(2,1)}, bf16[448,384]{1,0:T(8,128)(2,1)}, f32[96,1152]{1,0:T(8,128)}, f32[96,384]{1,0:T(8,128)}) custom-call(bf16[448,384]{1,0:T(8,128)(2,1)} %get-tuple-element.8.refs_0_, bf16[448,384]{1,0:T(8,128)(2,1)} %get-tuple-element.9.refs_1_, f32[96,1152]{1,0:T(8,128)} %get-tuple-element.10.refs_2_, ...), custom_call_target="tpu_custom_call" | custom-call | tf_op jit(solution)/shard_map/pallas_call | solution.py:800

commit v7 on v6

--- a/solution.py
+++ b/solution.py
@@ -394,6 +394,7 @@
     project(3)
     project(4)
 
+    gathered = len(sent)
     query_scale = qk_gain[0:1, :] * head_dim ** (-0.5)
     key_scale = qk_gain[1:2, :]
 
@@ -639,6 +640,9 @@
     have(-1)
     y_go(1)
     y_go(-1)
+    for copy in sent[:gathered]:
+        copy.wait_send()
+    del sent[:gathered]
     z_pass(1, 1, 2)
     z_take(1, 1, 1)
     z_take(0, 1, 1)

time: 146 us -> 145 us (level)
  no operation moved by 1% of the time
where the time goes in v7:
time: 145 us
  Pallas kernels  144 us (99%)
    pallas_call x1, Pallas kernels, branch(): pl.pallas_call(branch_kernel, out_shape=(jax.ShapeDtypeStruct((tok, share...  142 us

profile of v7, /device:TPU:2, one launch (start us, length us, event | category | flops | bytes accessed | tf_op | source)
XLA Modules:
  0.0 144.9 jit_solution(17843200655613909876)
XLA Ops:
  0.6 142.0 %shard_map.111 = (bf16[448,384]{1,0:T(8,128)(2,1)}, bf16[448,384]{1,0:T(8,128)(2,1)}, f32[96,1152]{1,0:T(8,128)}, f32[96,384]{1,0:T(8,128)}) custom-call(s32[4]{0:T(128)} %masks_ref.1, s32[4,32]{1,0:T(4,128)} %bitcast.3, f32[1,3072]{1,0:T(1,128)} %bitcast.2, f32[2,128]{1,0:T(2,128)} %qk_gain.1, bf16[448,3072]{1,0:T(8,128)(2,1)} %patches.1, ...), custom_call_target="tpu_custom_call" | custom-call | flops 12999999488 | bytes 16777216 | tf_op jit(solution)/shard_map/pallas_call | solution.py:737
  142.6 2.1 %shard_map.112 = (bf16[448,384]{1,0:T(8,128)(2,1)}, bf16[448,384]{1,0:T(8,128)(2,1)}, f32[96,1152]{1,0:T(8,128)}, f32[96,384]{1,0:T(8,128)}) custom-call(bf16[448,384]{1,0:T(8,128)(2,1)} %get-tuple-element.8.refs_0_, bf16[448,384]{1,0:T(8,128)(2,1)} %get-tuple-element.9.refs_1_, f32[96,1152]{1,0:T(8,128)} %get-tuple-element.10.refs_2_, ...), custom_call_target="tpu_custom_call" | custom-call | tf_op jit(solution)/shard_map/pallas_call | solution.py:804
